TPU v7x, 128 devices: a whole 4x4x4 slice. The times are simulated.
128 devices in a mesh: group: 8 (over z, x_hi), local: 16 (over x_lo, y, core).
Axes of the slice: x: 4 (x_hi: 2, x_lo: 2; x = x_hi * 2 + x_lo), y: 4, z: 4, core: 2. Of those that a mesh axis runs over, the one named last changes fastest.
Arguments:
- features: bfloat16 [262144, 512], P(('group', 'local')), may hold values from -6 to 6
- weight: bfloat16 [512, 512], replicated, may hold values from -0.25 to 0.25
- cotangent: bfloat16 [262144, 512], P(('group', 'local')), may hold values from -6 to 6
- tile_vals: bfloat16 [32768, 128, 128], P(('group', 'local')), may hold values from -0.125 to 0.125
- tile_rows: int32 [32768], P(('group', 'local')), may hold values from 0 to 15
- tile_cols: int32 [32768], P(('group', 'local')), may hold values from 0 to 47
- send_rows: int32 [128, 128, 32], P(('group', 'local')), may hold values from 0 to 2047, as said below
- counts: int32 [128, 128], P(('group', 'local')), may hold values from 1 to 32, as said below
Outputs:
- activated: bfloat16 [262144, 512], P(('group', 'local'))
- feature_grad: bfloat16 [262144, 512], P(('group', 'local'))
- weight_grad: float32 [512, 512], replicated
Inputs may be any that keep to these rules, and one draw needn't show every extreme that they name: Each list send_rows[s, d] holds 32 distinct local row numbers of device s. `counts`: some destinations are busy: every source sends them 32 rows; at least one such destination exists.
All inputs are finite; a program needn't handle non-finite values.
Results may differ from a plain program's by a relative error of at most 0.006.
Values may be sent and summed in bfloat16 or wider, within the bound.
A program may use at most 192 MiB of HBM per device.

v0:
```python
import math

import jax
import jax.numpy as jnp
from jax import lax
from jax.sharding import PartitionSpec as P


def per_device(features, weight, cotangent, tile_vals, tile_rows, tile_cols, send_rows, counts):
    rows_own, width = features.shape
    tile_edge = tile_vals.shape[1]
    num_tiles = tile_vals.shape[0]
    row_blocks = rows_own // tile_edge
    lists = send_rows[0]
    peers, slots = lists.shape
    live_slots = jnp.arange(slots)[None, :] < counts[0][:, None]
    outgoing = jnp.where(live_slots[..., None], features[lists], jnp.zeros((), features.dtype))
    arrived = lax.all_to_all(outgoing, ("group", "local"), split_axis=0, concat_axis=0, tiled=True)
    blocks = jnp.concatenate([features, arrived.reshape(peers * slots, width)], axis=0).reshape(
        -1, tile_edge, width
    )
    col_blocks = blocks.shape[0]
    col_ids = jnp.arange(col_blocks, dtype=jnp.int32)
    row_ids = jnp.arange(row_blocks, dtype=jnp.int32)
    batch_tiles = math.gcd(num_tiles, 32)
    turns = num_tiles // batch_tiles
    tile_batches = (
        tile_vals.reshape(turns, batch_tiles, tile_edge, tile_edge),
        tile_rows.reshape(turns, batch_tiles),
        tile_cols.reshape(turns, batch_tiles),
    )

    def gather_step(total, item):
        values, rows_of, cols_of = item
        select = (cols_of[:, None] == col_ids[None, :]).astype(jnp.bfloat16)
        picked = jnp.einsum(
            "tc,cjf->tjf", select, blocks, preferred_element_type=jnp.float32
        ).astype(jnp.bfloat16)
        product = jnp.einsum("tij,tjf->tif", values, picked, preferred_element_type=jnp.float32)
        target = (rows_of[:, None] == row_ids[None, :]).astype(jnp.float32)
        added = jnp.einsum(
            "tb,tif->bif",
            target,
            product,
            preferred_element_type=jnp.float32,
            precision=lax.Precision.HIGHEST,
        )
        return (total + added, None)

    summed, unused = lax.scan(
        gather_step, jnp.zeros((row_blocks, tile_edge, width), jnp.float32), tile_batches
    )
    hidden = summed.reshape(rows_own, width).astype(jnp.bfloat16)
    preact = jnp.dot(hidden, weight, preferred_element_type=jnp.float32)
    gate = jax.nn.sigmoid(preact)
    activated = (preact * gate).astype(jnp.bfloat16)
    slope = (cotangent.astype(jnp.float32) * gate * (1.0 + preact * (1.0 - gate))).astype(
        jnp.bfloat16
    )
    partial_grad = lax.dot_general(
        hidden, slope, (((0,), (0,)), ((), ())), preferred_element_type=jnp.float32
    )
    weight_grad = lax.psum(partial_grad, ("group", "local"))
    hidden_grad = lax.dot_general(
        slope, weight, (((1,), (1,)), ((), ())), preferred_element_type=jnp.float32
    )
    hidden_grad = hidden_grad.astype(jnp.bfloat16).reshape(row_blocks, tile_edge, width)

    def spread_step(total, item):
        values, rows_of, cols_of = item
        select = (rows_of[:, None] == row_ids[None, :]).astype(jnp.bfloat16)
        picked = jnp.einsum(
            "tb,bjf->tjf", select, hidden_grad, preferred_element_type=jnp.float32
        ).astype(jnp.bfloat16)
        product = jnp.einsum("tji,tjf->tif", values, picked, preferred_element_type=jnp.float32)
        target = (cols_of[:, None] == col_ids[None, :]).astype(jnp.float32)
        added = jnp.einsum(
            "tc,tif->cif",
            target,
            product,
            preferred_element_type=jnp.float32,
            precision=lax.Precision.HIGHEST,
        )
        return (total + added, None)

    spread, unused = lax.scan(
        spread_step, jnp.zeros((col_blocks, tile_edge, width), jnp.float32), tile_batches
    )
    spread = spread.reshape(-1, width)
    owned = spread[:rows_own]
    remote = spread[rows_own:].reshape(peers, slots, width)
    returned = lax.all_to_all(remote, ("group", "local"), split_axis=0, concat_axis=0, tiled=True)
    returned = jnp.where(live_slots[..., None], returned, jnp.float32(0.0))
    feature_grad = owned.at[lists.reshape(-1)].add(returned.reshape(-1, width))
    return (activated, feature_grad.astype(jnp.bfloat16), weight_grad)


def solution(mesh):
    return jax.shard_map(
        per_device,
        mesh=mesh,
        in_specs=(
            P(("group", "local"), None),
            P(),
            P(("group", "local"), None),
            P(("group", "local"), None, None),
            P(("group", "local")),
            P(("group", "local")),
            P(("group", "local"), None, None),
            P(("group", "local"), None),
        ),
        out_specs=(P(("group", "local"), None), P(("group", "local"), None), P()),
        check_vma=False,
    )
```

profile of v0, /device:TPU:39, one launch (start us, length us, event | category | flops | bytes accessed | tf_op | source)
XLA Modules:
  0.0 786.4 jit_solution(315825270758375095)
XLA Ops:
  8.9 19.2 %gather_fusion = bf16[4096,512]{1,0:T(8,128)(2,1)} fusion(bf16[2048,512]{1,0:T(8,128)(2,1)} %param.12, s32[4096]{0:T(1024)S(1)} %broadcast_clamp_fusion), kind=kCustom, calls=%fused_computation | custom fusion | bytes 8404992 | tf_op jit(solution)/shard_map/gather | solution.py:17
  28.2 3.9 broadcast_select_fusion.1
  32.0 11.0 %all-to-all-start = ((bf16[128,32,512]{2,1,0:T(8,128)(2,1)}), bf16[128,32,512]{2,1,0:T(8,128)(2,1)}, u32[]{:S(2)}, u32[]{:S(2)}) async-start(bf16[128,32,512]{2,1,0:T(8,128)(2,1)} %broadcast_select_fusion.1), calls=%async_computation | async-start | bytes 8388608 | tf_op jit(solution)/shard_map/all_to_all | solution.py:18
  43.2 49.4 %all-to-all-done = bf16[128,32,512]{2,1,0:T(8,128)(2,1)} async-done(((bf16[128,32,512]{2,1,0:T(8,128)(2,1)}), bf16[128,32,512]{2,1,0:T(8,128)(2,1)}, u32[]{:S(2)}, u32[]{:S(2)}) %all-to-all-start) | async-done | bytes 4194336 | tf_op jit(solution)/shard_map/all_to_all | solution.py:18
  92.6 5.2 pad_maximum_fusion
  97.8 220.4 %while.22 = (s32[]{:T(128)}, f32[16,128,512]{2,0,1:T(8,128)}, s32[8,32]{1,0:T(8,128)S(1)}, bf16[8,32,128,128]{3,2,1,0:T(8,128)(2,1)}, s32[8,32]{1,0:T(8,128)S(1)...) while((s32[]{:T(128)}, f32[16,128,512]{2,0,1:T(8,128)}, s32[8,32]{1,0:T(8,128)S(1)}, ...), condition=%wide.region_1.2_spmd.clone, body=%wide.region_0.1_spmd.clone.sunk | while | flops 1142949888 | bytes 74449824 | solution.py:50
  98.0 7.2 fusion.73
  105.2 6.5 fusion.74
  111.8 10.3 %select_add_fusion.4 = f32[16,128,512]{2,0,1:T(8,128)S(1)} fusion(f32[16,128,512]{2,0,1:T(8,128)S(1)} %copy-done.3, f32[32,128,512]{2,1,0:T(8,128)S(1)} %fusion.74, pred[]{:T(512)S(6)} %compare.6, s32[32]{0:T(128)S(1)} %get-tuple-element.242), kind=kOutput, calls=%fused_computation.12.clone.1 | convolution fusion | flops 404750848 | bytes 16777344 | tf_op jit(solution)/shard_map/while/body/eval_jaxpr/tb,tif->bif/dot_general | solution.py:41
  122.1 2.0 copy-done.4
  124.1 7.2 fusion.73
  131.3 6.5 fusion.74
  137.9 10.3 %select_add_fusion.4 = f32[16,128,512]{2,0,1:T(8,128)S(1)} fusion(f32[16,128,512]{2,0,1:T(8,128)S(1)} %copy-done.3, f32[32,128,512]{2,1,0:T(8,128)S(1)} %fusion.74, pred[]{:T(512)S(6)} %compare.6, s32[32]{0:T(128)S(1)} %get-tuple-element.242), kind=kOutput, calls=%fused_computation.12.clone.1 | convolution fusion | flops 404750848 | bytes 16777344 | tf_op jit(solution)/shard_map/while/body/eval_jaxpr/tb,tif->bif/dot_general | solution.py:41
  148.2 2.0 copy-done.4
  150.3 7.2 fusion.73
  157.5 6.5 fusion.74
  164.0 10.3 %select_add_fusion.4 = f32[16,128,512]{2,0,1:T(8,128)S(1)} fusion(f32[16,128,512]{2,0,1:T(8,128)S(1)} %copy-done.3, f32[32,128,512]{2,1,0:T(8,128)S(1)} %fusion.74, pred[]{:T(512)S(6)} %compare.6, s32[32]{0:T(128)S(1)} %get-tuple-element.242), kind=kOutput, calls=%fused_computation.12.clone.1 | convolution fusion | flops 404750848 | bytes 16777344 | tf_op jit(solution)/shard_map/while/body/eval_jaxpr/tb,tif->bif/dot_general | solution.py:41
  174.3 2.0 copy-done.4
  176.4 7.2 fusion.73
  183.6 6.5 fusion.74
  190.1 10.3 %select_add_fusion.4 = f32[16,128,512]{2,0,1:T(8,128)S(1)} fusion(f32[16,128,512]{2,0,1:T(8,128)S(1)} %copy-done.3, f32[32,128,512]{2,1,0:T(8,128)S(1)} %fusion.74, pred[]{:T(512)S(6)} %compare.6, s32[32]{0:T(128)S(1)} %get-tuple-element.242), kind=kOutput, calls=%fused_computation.12.clone.1 | convolution fusion | flops 404750848 | bytes 16777344 | tf_op jit(solution)/shard_map/while/body/eval_jaxpr/tb,tif->bif/dot_general | solution.py:41
  202.5 7.2 fusion.73
  209.7 6.5 fusion.74
  216.3 10.3 %select_add_fusion.4 = f32[16,128,512]{2,0,1:T(8,128)S(1)} fusion(f32[16,128,512]{2,0,1:T(8,128)S(1)} %copy-done.3, f32[32,128,512]{2,1,0:T(8,128)S(1)} %fusion.74, pred[]{:T(512)S(6)} %compare.6, s32[32]{0:T(128)S(1)} %get-tuple-element.242), kind=kOutput, calls=%fused_computation.12.clone.1 | convolution fusion | flops 404750848 | bytes 16777344 | tf_op jit(solution)/shard_map/while/body/eval_jaxpr/tb,tif->bif/dot_general | solution.py:41
  228.6 7.2 fusion.73
  235.8 6.5 fusion.74
  242.4 10.3 %select_add_fusion.4 = f32[16,128,512]{2,0,1:T(8,128)S(1)} fusion(f32[16,128,512]{2,0,1:T(8,128)S(1)} %copy-done.3, f32[32,128,512]{2,1,0:T(8,128)S(1)} %fusion.74, pred[]{:T(512)S(6)} %compare.6, s32[32]{0:T(128)S(1)} %get-tuple-element.242), kind=kOutput, calls=%fused_computation.12.clone.1 | convolution fusion | flops 404750848 | bytes 16777344 | tf_op jit(solution)/shard_map/while/body/eval_jaxpr/tb,tif->bif/dot_general | solution.py:41
  254.8 7.2 fusion.73
  262.0 6.5 fusion.74
  268.5 10.3 %select_add_fusion.4 = f32[16,128,512]{2,0,1:T(8,128)S(1)} fusion(f32[16,128,512]{2,0,1:T(8,128)S(1)} %copy-done.3, f32[32,128,512]{2,1,0:T(8,128)S(1)} %fusion.74, pred[]{:T(512)S(6)} %compare.6, s32[32]{0:T(128)S(1)} %get-tuple-element.242), kind=kOutput, calls=%fused_computation.12.clone.1 | convolution fusion | flops 404750848 | bytes 16777344 | tf_op jit(solution)/shard_map/while/body/eval_jaxpr/tb,tif->bif/dot_general | solution.py:41
  280.9 7.2 fusion.73
  288.1 6.5 fusion.74
  294.6 10.3 %select_add_fusion.4 = f32[16,128,512]{2,0,1:T(8,128)S(1)} fusion(f32[16,128,512]{2,0,1:T(8,128)S(1)} %copy-done.3, f32[32,128,512]{2,1,0:T(8,128)S(1)} %fusion.74, pred[]{:T(512)S(6)} %compare.6, s32[32]{0:T(128)S(1)} %get-tuple-element.242), kind=kOutput, calls=%fused_computation.12.clone.1 | convolution fusion | flops 404750848 | bytes 16777344 | tf_op jit(solution)/shard_map/while/body/eval_jaxpr/tb,tif->bif/dot_general | solution.py:41
  318.2 4.6 copy.40
  322.8 3.6 multiply_convert_fusion
  327.8 195.9 %while.23 = (s32[]{:T(128)}, f32[48,128,512]{2,0,1:T(8,128)}, s32[8,32]{1,0:T(8,128)S(1)}, bf16[8,32,128,128]{3,2,1,0:T(8,128)(2,1)}, s32[8,32]{1,0:T(8,128)S(1)...) while((s32[]{:T(128)}, f32[48,128,512]{2,0,1:T(8,128)}, s32[8,32]{1,0:T(8,128)S(1)}, ...), condition=%wide.region_3.4_spmd.clone, body=%wide.region_2.3_spmd.clone.sunk | while | flops 1818232832 | bytes 53478252 | solution.py:86
  329.3 6.5 fusion.82
  335.8 14.0 %select_add_fusion.5 = f32[48,128,512]{2,0,1:T(8,128)} fusion(f32[48,128,512]{2,0,1:T(8,128)} %get-tuple-element.284, pred[]{:T(512)S(6)} %compare.7, f32[32,128,512]{2,1,0:T(8,128)S(1)} %fusion.82, s32[32]{0:T(128)S(1)} %get-tuple-element.250), kind=kOutput, calls=%fused_computation.26.clone.1 | convolution fusion | flops 1214252544 | bytes 33554560 | tf_op jit(solution)/shard_map/while/body/eval_jaxpr/tc,tif->cif/dot_general | solution.py:77
  351.4 6.5 fusion.82
  357.9 16.8 %select_add_fusion.5 = f32[48,128,512]{2,0,1:T(8,128)} fusion(f32[48,128,512]{2,0,1:T(8,128)} %get-tuple-element.284, pred[]{:T(512)S(6)} %compare.7, f32[32,128,512]{2,1,0:T(8,128)S(1)} %fusion.82, s32[32]{0:T(128)S(1)} %get-tuple-element.250), kind=kOutput, calls=%fused_computation.26.clone.1 | convolution fusion | flops 1214252544 | bytes 33554560 | tf_op jit(solution)/shard_map/while/body/eval_jaxpr/tc,tif->cif/dot_general | solution.py:77
  376.2 6.5 fusion.82
  382.7 16.8 %select_add_fusion.5 = f32[48,128,512]{2,0,1:T(8,128)} fusion(f32[48,128,512]{2,0,1:T(8,128)} %get-tuple-element.284, pred[]{:T(512)S(6)} %compare.7, f32[32,128,512]{2,1,0:T(8,128)S(1)} %fusion.82, s32[32]{0:T(128)S(1)} %get-tuple-element.250), kind=kOutput, calls=%fused_computation.26.clone.1 | convolution fusion | flops 1214252544 | bytes 33554560 | tf_op jit(solution)/shard_map/while/body/eval_jaxpr/tc,tif->cif/dot_general | solution.py:77
  401.0 6.5 fusion.82
  407.5 16.8 %select_add_fusion.5 = f32[48,128,512]{2,0,1:T(8,128)} fusion(f32[48,128,512]{2,0,1:T(8,128)} %get-tuple-element.284, pred[]{:T(512)S(6)} %compare.7, f32[32,128,512]{2,1,0:T(8,128)S(1)} %fusion.82, s32[32]{0:T(128)S(1)} %get-tuple-element.250), kind=kOutput, calls=%fused_computation.26.clone.1 | convolution fusion | flops 1214252544 | bytes 33554560 | tf_op jit(solution)/shard_map/while/body/eval_jaxpr/tc,tif->cif/dot_general | solution.py:77
  425.8 6.5 fusion.82
  432.3 16.8 %select_add_fusion.5 = f32[48,128,512]{2,0,1:T(8,128)} fusion(f32[48,128,512]{2,0,1:T(8,128)} %get-tuple-element.284, pred[]{:T(512)S(6)} %compare.7, f32[32,128,512]{2,1,0:T(8,128)S(1)} %fusion.82, s32[32]{0:T(128)S(1)} %get-tuple-element.250), kind=kOutput, calls=%fused_computation.26.clone.1 | convolution fusion | flops 1214252544 | bytes 33554560 | tf_op jit(solution)/shard_map/while/body/eval_jaxpr/tc,tif->cif/dot_general | solution.py:77
  450.6 6.5 fusion.82
  457.1 16.8 %select_add_fusion.5 = f32[48,128,512]{2,0,1:T(8,128)} fusion(f32[48,128,512]{2,0,1:T(8,128)} %get-tuple-element.284, pred[]{:T(512)S(6)} %compare.7, f32[32,128,512]{2,1,0:T(8,128)S(1)} %fusion.82, s32[32]{0:T(128)S(1)} %get-tuple-element.250), kind=kOutput, calls=%fused_computation.26.clone.1 | convolution fusion | flops 1214252544 | bytes 33554560 | tf_op jit(solution)/shard_map/while/body/eval_jaxpr/tc,tif->cif/dot_general | solution.py:77
  475.4 6.5 fusion.82
  481.9 16.8 %select_add_fusion.5 = f32[48,128,512]{2,0,1:T(8,128)} fusion(f32[48,128,512]{2,0,1:T(8,128)} %get-tuple-element.284, pred[]{:T(512)S(6)} %compare.7, f32[32,128,512]{2,1,0:T(8,128)S(1)} %fusion.82, s32[32]{0:T(128)S(1)} %get-tuple-element.250), kind=kOutput, calls=%fused_computation.26.clone.1 | convolution fusion | flops 1214252544 | bytes 33554560 | tf_op jit(solution)/shard_map/while/body/eval_jaxpr/tc,tif->cif/dot_general | solution.py:77
  500.2 6.5 fusion.82
  506.7 16.8 %select_add_fusion.5 = f32[48,128,512]{2,0,1:T(8,128)} fusion(f32[48,128,512]{2,0,1:T(8,128)} %get-tuple-element.284, pred[]{:T(512)S(6)} %compare.7, f32[32,128,512]{2,1,0:T(8,128)S(1)} %fusion.82, s32[32]{0:T(128)S(1)} %get-tuple-element.250), kind=kOutput, calls=%fused_computation.26.clone.1 | convolution fusion | flops 1214252544 | bytes 33554560 | tf_op jit(solution)/shard_map/while/body/eval_jaxpr/tc,tif->cif/dot_general | solution.py:77
  523.6 16.4 %copy.16 = f32[48,128,512]{2,1,0:T(8,128)} copy(f32[48,128,512]{2,0,1:T(8,128)} %get-tuple-element.88) | data formatting | bytes 25165824 | tf_op jit(solution)/shard_map/while | solution.py:86
  540.0 8.2 %slice.15 = f32[32,128,512]{2,1,0:T(8,128)} slice(f32[48,128,512]{2,1,0:T(8,128)} %copy.16), slice={[16:48], [0:128], [0:512]} | slice | bytes 16777216 | tf_op jit(solution)/shard_map/slice | solution.py:91
  548.2 9.0 %all-to-all-start.1 = ((f32[128,32,512]{2,1,0:T(8,128)}), f32[128,32,512]{2,1,0:T(8,128)}, u32[]{:S(2)}, u32[]{:S(2)}) async-start(f32[128,32,512]{2,1,0:T(8,128)} %bitcast.67), calls=%async_computation.1 | async-start | bytes 16777216 | tf_op jit(solution)/shard_map/all_to_all | solution.py:92
  557.8 5.2 slice.10
  563.0 2.2 fusion.44
  565.2 6.6 copy.14
  571.8 82.6 %all-to-all-done.1 = f32[128,32,512]{2,1,0:T(8,128)} async-done(((f32[128,32,512]{2,1,0:T(8,128)}), f32[128,32,512]{2,1,0:T(8,128)}, u32[]{:S(2)}, u32[]{:S(2)}) %all-to-all-start.1) | async-done | bytes 8388640 | tf_op jit(solution)/shard_map/all_to_all | solution.py:92
  654.5 5.9 broadcast_select_fusion
  660.3 29.3 %scatter_fusion = f32[2048,512]{1,0:T(8,128)} fusion(f32[2048,512]{1,0:T(8,128)} %bitcast.63, s32[4096]{0:T(1024)S(1)} %bitcast.72, f32[4096,512]{1,0:T(8,128)} %bitcast.66), kind=kCustom, calls=%fused_computation.1 | custom fusion | flops 2097152 | bytes 25182208 | tf_op jit(solution)/shard_map/scatter-add | solution.py:94
  689.7 3.8 convert_element_type.37
  693.5 83.4 %all-reduce.2.cloned.1.call-done = f32[512,512]{1,0:T(8,128)} async-done(((f32[512,512]{1,0:T(8,128)}), f32[512,512]{1,0:T(8,128)}) %all-reduce.2.cloned.1.call-update) | async-done | bytes 1048592 | tf_op jit(solution)/shard_map/psum | solution.py:63
  776.9 2.3 copy.67
  (94 shorter events, 26.5 us)
Async XLA Ops:
  7.2 315.6 %copy-start = (bf16[512,512]{1,0:T(8,128)(2,1)S(1)}, bf16[512,512]{1,0:T(8,128)(2,1)}, u32[]{:S(2)}) copy-start(bf16[512,512]{1,0:T(8,128)(2,1)} %param.13) | copy-start | bytes 1572868
  8.0 20.2 %copy-start.7 = (pred[128,32]{1,0:T(8,128)(4,1)}, pred[128,32]{1,0:T(8,128)(4,1)S(1)}, u32[]{:S(2)}) copy-start(pred[128,32]{1,0:T(8,128)(4,1)S(1)} %iota_compare_fusion.4) | copy-start | bytes 12292
  32.0 11.0 %copy-start.10 = (s32[256]{0:T(256)S(1)}, s32[256]{0:T(256)}, u32[]{:S(2)}) copy-start(s32[256]{0:T(256)} %param.16) | copy-start | bytes 3076
  32.0 11.1 %copy-start.11 = (s32[256]{0:T(256)S(1)}, s32[256]{0:T(256)}, u32[]{:S(2)}) copy-start(s32[256]{0:T(256)} %param.17) | copy-start | bytes 3076
  32.0 60.5 %copy-start.2 = (bf16[2048,512]{1,0:T(8,128)(2,1)S(1)}, bf16[2048,512]{1,0:T(8,128)(2,1)}, u32[]{:S(2)}) copy-start(bf16[2048,512]{1,0:T(8,128)(2,1)} %param.12) | copy-start | bytes 6291460
  32.0 60.5 %all-to-all-start = ((bf16[128,32,512]{2,1,0:T(8,128)(2,1)}), bf16[128,32,512]{2,1,0:T(8,128)(2,1)}, u32[]{:S(2)}, u32[]{:S(2)}) async-start(bf16[128,32,512]{2,1,0:T(8,128)(2,1)} %broadcast_select_fusion.1), calls=%async_computation | async-start | bytes 8388608 | tf_op jit(solution)/shard_map/all_to_all | solution.py:18
  105.2 6.6 copy-start.3
  122.1 2.1 copy-start.4
  131.3 6.6 copy-start.3
  148.2 2.1 copy-start.4
  157.5 6.6 copy-start.3
  174.3 2.1 copy-start.4
  183.6 6.6 copy-start.3
  200.4 2.1 copy-start.4
  209.7 6.6 copy-start.3
  226.6 2.1 copy-start.4
  235.8 6.6 copy-start.3
  252.7 2.1 copy-start.4
  261.9 6.6 copy-start.3
  278.8 2.1 copy-start.4
  288.1 6.6 copy-start.3
  304.9 2.1 copy-start.4
  318.2 4.6 copy-start.12
  322.8 3.7 copy-start.5
  326.4 1.4 copy-start.13
  548.2 9.3 %copy-start.9 = (s32[1,128,32]{1,2,0:T(8,128)S(1)}, s32[1,128,32]{1,2,0:T(8,128)}, u32[]{:S(2)}) copy-start(s32[1,128,32]{1,2,0:T(8,128)} %param.18) | copy-start | bytes 49156
  548.2 106.3 %all-to-all-start.1 = ((f32[128,32,512]{2,1,0:T(8,128)}), f32[128,32,512]{2,1,0:T(8,128)}, u32[]{:S(2)}, u32[]{:S(2)}) async-start(f32[128,32,512]{2,1,0:T(8,128)} %bitcast.67), calls=%async_computation.1 | async-start | bytes 16777216 | tf_op jit(solution)/shard_map/all_to_all | solution.py:92
  557.2 219.7 %all-reduce.2.cloned.1.call-start = ((), (), s32[]{:S(2)}) async-start(), calls=%async_computation.2 | async-start | bytes 2097152 | tf_op jit(solution)/shard_map/psum | solution.py:63
  557.7 5.2 copy-start.6
  557.8 5.2 copy-start.14
  565.2 89.2 %copy-start.8 = (pred[128,32]{1,0:T(8,128)(4,1)S(1)}, pred[128,32]{1,0:T(8,128)(4,1)}, u32[]{:S(2)}) copy-start(pred[128,32]{1,0:T(8,128)(4,1)} %copy-done.7) | copy-start | bytes 12292
  660.3 118.8 %copy-start.1 = (bf16[512,512]{1,0:T(8,128)(2,1)S(1)}, bf16[512,512]{1,0:T(8,128)(2,1)}, u32[]{:S(2)}) copy-start(bf16[512,512]{1,0:T(8,128)(2,1)} %param.13) | copy-start | bytes 1572868
Sparse Core Ops, SparseCore 0:
  565.4 211.4 all-reduce.1
where the time goes:
time: 792 us; the launch traced here: 786 us
  matrix products  395 us (50%)
  waiting for transfers between devices  215 us (27%)
  local copies, waits for them, and re-layouts  79.5 us (10%)
  other arithmetic  49.6 us (6%)
  starting transfers between devices  20.3 us (3%)
  between operations  14.7 us (2%)
  loops' own time  12 us (2%)
    dot_general x8, matrix products, spread_step(): jnp.einsum('tc,tif->cif', target, product, preferred_element_type=jnp.flo...  131 us
    psum x1, waiting for transfers between devices, per_device(): weight_grad = lax.psum(partial_grad, ('group', 'local'))  83.4 us
    all_to_all x1, waiting for transfers between devices, per_device(): lax.all_to_all(remote, ('group', 'local'), split_axis=0, concat_axis=0, t...  82.6 us
    dot_general x8, matrix products, gather_step(): jnp.einsum('tb,tif->bif', target, product, preferred_element_type=jnp.flo...  82.4 us
    dot_general x8, matrix products, gather_step(): jnp.einsum('tc,cjf->tjf', select, blocks, preferred_element_type=jnp.floa...  57.5 us
    dot_general x8, matrix products, gather_step(): jnp.einsum('tij,tjf->tif', values, picked, preferred_element_type=jnp.flo...  52.3 us
    dot_general x8, matrix products, spread_step(): jnp.einsum('tji,tjf->tif', values, picked, preferred_element_type=jnp.flo...  51.8 us
    all_to_all x1, waiting for transfers between devices, per_device(): lax.all_to_all(outgoing, ('group', 'local'), split_axis=0, concat_axis=0,...  49.4 us
  transfers between devices with their start and end apart: 3, of which 3 were waited for; matrix products, arithmetic and copies ran while one was open for 7% of the time, Pallas kernels for 0%

commit v1 on v0

v1 whole, which is shorter than its diff:
```python
import functools

import jax
import jax.numpy as jnp
from jax import lax
from jax.experimental import pallas as pl
from jax.experimental.pallas import tpu as pltpu
from jax.sharding import PartitionSpec as P

MESH = pl.DeviceIdType.MESH
F32 = jnp.float32
BF16 = jnp.bfloat16
VMEM_LIMIT = 60 * 1024 * 1024


def place(groups, locals_):
    g = lax.axis_index("group")
    l = lax.axis_index("local")
    return g, l, g * locals_ + l


def greet_all(groups, locals_):
    g, l, me = place(groups, locals_)
    barrier = pltpu.get_barrier_semaphore()

    @pl.loop(1, groups * locals_)
    def _(k):
        peer = lax.rem(me + k, groups * locals_)
        pl.semaphore_signal(
            barrier,
            inc=1,
            device_id=(lax.div(peer, locals_), lax.rem(peer, locals_)),
            device_id_type=MESH,
        )

    pl.semaphore_wait(barrier, groups * locals_ - 1)


def wait_rows(ref, rows, sem):
    view = ref.at[pl.ds(0, rows)]
    pltpu.make_async_copy(view, view, sem).wait()


def exchange_kernel(groups, locals_, slots, feat, idx, arrived, outgoing, send_sem, recv_sem, own_sem):
    g, l, me = place(groups, locals_)
    batch = locals_ * slots
    rows_own = feat.shape[0]
    greet_all(groups, locals_)

    def send_group(step, first):
        dest_g = lax.rem(g + groups - step, groups)
        base = dest_g * batch
        picks = idx[pl.ds(base, batch), :]
        cols = lax.broadcasted_iota(jnp.int32, (batch, rows_own), 1)
        onehot = (picks == cols).astype(F32).astype(BF16)
        rows = jnp.dot(onehot, feat[...], preferred_element_type=F32)
        outgoing[pl.ds(base, batch), :] = rows.astype(BF16)

        @pl.loop(1 if first else 0, locals_)
        def _(i):
            dest_l = lax.rem(l + i, locals_)
            pltpu.make_async_remote_copy(
                src_ref=outgoing.at[pl.ds(base + dest_l * slots, slots)],
                dst_ref=arrived.at[pl.ds(me * slots, slots)],
                send_sem=send_sem.at[step],
                recv_sem=recv_sem.at[step],
                device_id=(dest_g, dest_l),
                device_id_type=MESH,
            ).start()

    send_group(0, True)
    own = pltpu.make_async_copy(
        outgoing.at[pl.ds(me * slots, slots)], arrived.at[pl.ds(me * slots, slots)], own_sem
    )
    own.start()

    @pl.loop(1, groups)
    def _(step):
        send_group(step, False)

    own.wait()
    wait_rows(outgoing, batch - slots, send_sem.at[0])
    wait_rows(arrived, batch - slots, recv_sem.at[0])

    @pl.loop(1, groups)
    def _(step):
        wait_rows(outgoing, batch, send_sem.at[step])
        wait_rows(arrived, batch, recv_sem.at[step])


def layer_kernel(
    order_f, start_f, order_b, start_b,
    feat, arrived, vals, weight, cot,
    activated, wgrad, remote, owned,
    vbuf, xbuf, cotbuf, wbuf, actbuf, hidden, hgrad, slope, acc, rembuf, ownbuf, sems,
):
    tiles, edge, _ = vals.shape
    rows_own, width = feat.shape
    row_blocks = rows_own // edge
    col_blocks = xbuf.shape[0] // edge
    loads = [
        pltpu.make_async_copy(feat, xbuf.at[pl.ds(0, rows_own)], sems.at[0]),
        pltpu.make_async_copy(arrived, xbuf.at[pl.ds(rows_own, xbuf.shape[0] - rows_own)], sems.at[1]),
        pltpu.make_async_copy(vals, vbuf.at[pl.ds(0, tiles)], sems.at[2]),
        pltpu.make_async_copy(cot, cotbuf, sems.at[3]),
        pltpu.make_async_copy(weight, wbuf, sems.at[4]),
    ]
    for load in loads:
        load.start()
    vbuf[tiles] = jnp.zeros((edge, edge), BF16)
    for load in loads:
        load.wait()

    depth = 4

    def tile_of(order, at, end):
        return jnp.where(at < end, order[jnp.minimum(at, tiles - 1)], tiles)

    @pl.loop(0, row_blocks)
    def _(r):
        begin, end = start_f[r], start_f[r + 1]
        acc[...] = jnp.zeros_like(acc)

        @pl.loop(0, lax.div(end - begin + depth - 1, depth))
        def _(q):
            left, right = [], []
            for k in range(depth):
                at = begin + q * depth + k
                t = tile_of(order_f, at, end)
                packed = order_f[tiles + jnp.minimum(at, tiles - 1)]
                left.append(vbuf[t])
                right.append(xbuf[pl.ds(pl.multiple_of(packed * edge, edge), edge), :])
            acc[...] += jnp.dot(
                jnp.concatenate(left, axis=1),
                jnp.concatenate(right, axis=0),
                preferred_element_type=F32,
            )

        hidden[pl.ds(pl.multiple_of(r * edge, edge), edge), :] = acc[...].astype(BF16)

    wgrad[...] = jnp.zeros_like(wgrad)
    band = 512

    @pl.loop(0, rows_own // band)
    def _(b):
        at = pl.ds(pl.multiple_of(b * band, band), band)
        h = hidden[at, :]
        pre = jnp.dot(h, wbuf[...], preferred_element_type=F32)
        gate = jax.nn.sigmoid(pre)
        actbuf[at, :] = (pre * gate).astype(BF16)
        s = (cotbuf[at, :].astype(F32) * gate * (1.0 + pre * (1.0 - gate))).astype(BF16)
        hgrad[at, :] = lax.dot_general(
            s, wbuf[...], (((1,), (1,)), ((), ())), preferred_element_type=F32
        ).astype(BF16)
        wgrad[...] += lax.dot_general(h, s, (((0,), (0,)), ((), ())), preferred_element_type=F32)

    save_act = pltpu.make_async_copy(actbuf, activated, sems.at[0])
    save_act.start()

    def spread_block(c):
        begin, end = start_b[c], start_b[c + 1]
        acc[...] = jnp.zeros_like(acc)

        @pl.loop(0, lax.div(end - begin + 1, 2))
        def _(q):
            left, right = [], []
            for k in range(2):
                at = begin + q * 2 + k
                t = tile_of(order_b, at, end)
                r = order_b[tiles + jnp.minimum(at, tiles - 1)]
                left.append(vbuf[t])
                right.append(hgrad[pl.ds(pl.multiple_of(r * edge, edge), edge), :])
            acc[...] += lax.dot_general(
                jnp.concatenate(left, axis=0),
                jnp.concatenate(right, axis=0),
                (((0,), (0,)), ((), ())),
                preferred_element_type=F32,
            )

    @pl.loop(row_blocks, col_blocks)
    def _(c):
        spread_block(c)
        rembuf[pl.ds(pl.multiple_of((c - row_blocks) * edge, edge), edge), :] = acc[...].astype(BF16)

    save_rem = pltpu.make_async_copy(rembuf, remote, sems.at[1])
    save_rem.start()

    @pl.loop(0, row_blocks)
    def _(c):
        spread_block(c)
        ownbuf[pl.ds(pl.multiple_of(c * edge, edge), edge), :] = acc[...]

    save_own = pltpu.make_async_copy(ownbuf, owned, sems.at[2])
    save_own.start()
    save_act.wait()
    save_rem.wait()
    save_own.wait()


def return_kernel(
    groups, locals_, slots,
    remote, owned, idx, part,
    grad, wgrad,
    returned, total, wsum, sib, chunks, gathered,
    send_sem, recv_sem, own_sems, sib_send, sib_recv, rs_send, rs_recv, ag_send, ag_recv,
):
    g, l, me = place(groups, locals_)
    batch = locals_ * slots
    rows_own, width = total.shape
    core = lax.rem(l, 2)
    mates = locals_ // 2
    chips = groups * mates
    chip = g * mates + lax.div(l, 2)
    half = part.shape[0] // 2
    edge_r, edge_c = chunks.shape[1:]
    across = width // edge_c

    load_own = pltpu.make_async_copy(owned, total, own_sems.at[0])
    load_own.start()
    keep = pltpu.make_async_copy(
        remote.at[pl.ds(me * slots, slots)], returned.at[pl.ds(me * slots, slots)], own_sems.at[1]
    )
    keep.start()
    greet_all(groups, locals_)

    mine = pl.multiple_of(core * half, half)
    other = pl.multiple_of((1 - core) * half, half)
    sibling = (g, l + 1 - 2 * core)
    swap = pltpu.make_async_remote_copy(
        src_ref=part.at[pl.ds(other, half)],
        dst_ref=sib,
        send_sem=sib_send.at[0],
        recv_sem=sib_recv.at[0],
        device_id=sibling,
        device_id_type=MESH,
    )
    swap.start()

    def send_group(step, first):
        dest_g = lax.rem(g + groups - step, groups)
        base = dest_g * batch

        @pl.loop(1 if first else 0, locals_)
        def _(i):
            dest_l = lax.rem(l + i, locals_)
            pltpu.make_async_remote_copy(
                src_ref=remote.at[pl.ds(base + dest_l * slots, slots)],
                dst_ref=returned.at[pl.ds(me * slots, slots)],
                send_sem=send_sem.at[step],
                recv_sem=recv_sem.at[step],
                device_id=(dest_g, dest_l),
                device_id_type=MESH,
            ).start()

    def spot(q):
        return lax.div(q, across) * edge_r, lax.rem(q, across) * edge_c

    def peer_of(q):
        return (lax.div(q, mates), 2 * lax.rem(q, mates) + core)

    swap.wait()
    wsum[...] = part[pl.ds(mine, half), :] + sib[...]

    @pl.loop(1, chips)
    def _(k):
        q = lax.rem(chip + k, chips)
        r0, c0 = spot(q)
        pltpu.make_async_remote_copy(
            src_ref=wsum.at[pl.ds(pl.multiple_of(r0, edge_r), edge_r), pl.ds(pl.multiple_of(c0, edge_c), edge_c)],
            dst_ref=chunks.at[chip],
            send_sem=rs_send,
            recv_sem=rs_recv,
            device_id=peer_of(q),
            device_id_type=MESH,
        ).start()

    send_group(0, True)

    @pl.loop(1, groups)
    def _(step):
        send_group(step, False)

    r0, c0 = spot(chip)
    here = (pl.ds(pl.multiple_of(r0, edge_r), edge_r), pl.ds(pl.multiple_of(c0, edge_c), edge_c))
    chunks[chip] = wsum[here[0], here[1]]
    wait_rows(chunks, chips - 1, rs_send)
    wait_rows(chunks, chips - 1, rs_recv)
    gathered[...] = jnp.sum(chunks[...], axis=0)
    there = (pl.ds(pl.multiple_of(mine + r0, edge_r), edge_r), here[1])
    wgrad[there[0], there[1]] = gathered[...]

    @pl.loop(1, chips)
    def _(k):
        q = lax.rem(chip + k, chips)
        pltpu.make_async_remote_copy(
            src_ref=gathered,
            dst_ref=wgrad.at[there[0], there[1]],
            send_sem=ag_send,
            recv_sem=ag_recv,
            device_id=peer_of(q),
            device_id_type=MESH,
        ).start()

    load_own.wait()
    keep.wait()

    def add_group(step):
        src_g = lax.rem(g + step, groups)
        base = pl.multiple_of(src_g * batch, batch)
        picks = idx[:, pl.ds(base, batch)]
        rows = returned[pl.ds(base, batch), :]
        band = 512

        @pl.loop(0, rows_own // band)
        def _(b):
            at = pl.multiple_of(b * band, band)
            ids = lax.broadcasted_iota(jnp.int32, (band, batch), 0) + at
            onehot = (ids == picks).astype(F32).astype(BF16)
            total[pl.ds(at, band), :] += jnp.dot(onehot, rows, preferred_element_type=F32)

    wait_rows(returned, batch - slots, recv_sem.at[0])
    add_group(0)

    @pl.loop(1, groups)
    def _(step):
        wait_rows(returned, batch, recv_sem.at[step])
        add_group(step)

    wait_rows(chunks, chips - 1, ag_send)
    wait_rows(chunks, chips - 1, ag_recv)
    back = pltpu.make_async_remote_copy(
        src_ref=wgrad.at[pl.ds(mine, half)],
        dst_ref=wgrad.at[pl.ds(mine, half)],
        send_sem=sib_send.at[1],
        recv_sem=sib_recv.at[1],
        device_id=sibling,
        device_id_type=MESH,
    )
    back.start()
    grad[...] = total[...].astype(BF16)
    wait_rows(returned, batch - slots, send_sem.at[0])

    @pl.loop(1, groups)
    def _(step):
        wait_rows(returned, batch, send_sem.at[step])

    back.wait()


def ordered(keys, mates, buckets):
    n = keys.shape[0]
    ids = jnp.arange(n, dtype=jnp.int32)
    full = keys * n + ids
    rank = jnp.sum((full[None, :] < full[:, None]).astype(jnp.int32), axis=1)
    hit = rank[:, None] == ids[None, :]
    order = jnp.sum(jnp.where(hit, ids[:, None], 0), axis=0)
    paired = jnp.sum(jnp.where(hit, mates[:, None], 0), axis=0)
    starts = jnp.sum((keys[None, :] < jnp.arange(buckets + 1, dtype=jnp.int32)[:, None]).astype(jnp.int32), axis=1)
    return jnp.concatenate([order, paired]), starts


def per_device(groups, locals_, features, weight, cotangent, tile_vals, tile_rows, tile_cols, send_rows, counts):
    rows_own, width = features.shape
    tiles, edge, _ = tile_vals.shape
    peers, slots = send_rows.shape[1:]
    row_blocks = rows_own // edge
    remote_rows = peers * slots
    col_blocks = (rows_own + remote_rows) // edge
    live = jnp.arange(slots, dtype=jnp.int32)[None, :] < counts[0][:, None]
    idx = jnp.where(live, send_rows[0], -1)
    any_ = pl.BlockSpec(memory_space=pl.ANY)
    vmem = pl.BlockSpec(memory_space=pltpu.VMEM)
    smem = pl.BlockSpec(memory_space=pltpu.SMEM)
    order_f, start_f = ordered(tile_rows, tile_cols, row_blocks)
    order_b, start_b = ordered(tile_cols, tile_rows, col_blocks)

    arrived = pl.pallas_call(
        functools.partial(exchange_kernel, groups, locals_, slots),
        out_shape=jax.ShapeDtypeStruct((remote_rows, width), BF16),
        in_specs=[vmem, vmem],
        out_specs=any_,
        scratch_shapes=[
            pltpu.VMEM((remote_rows, width), BF16),
            pltpu.SemaphoreType.DMA((groups,)),
            pltpu.SemaphoreType.DMA((groups,)),
            pltpu.SemaphoreType.DMA,
        ],
        compiler_params=pltpu.CompilerParams(
            collective_id=0, has_side_effects=True, vmem_limit_bytes=VMEM_LIMIT
        ),
        name="exchange",
    )(features, idx.reshape(remote_rows, 1))

    activated, part, remote, owned = pl.pallas_call(
        layer_kernel,
        out_shape=(
            jax.ShapeDtypeStruct((rows_own, width), BF16),
            jax.ShapeDtypeStruct((width, width), F32),
            jax.ShapeDtypeStruct((remote_rows, width), BF16),
            jax.ShapeDtypeStruct((rows_own, width), F32),
        ),
        in_specs=[smem] * 4 + [any_] * 5,
        out_specs=(any_, vmem, any_, any_),
        scratch_shapes=[
            pltpu.VMEM((tiles + 1, edge, edge), BF16),
            pltpu.VMEM((rows_own + remote_rows, width), BF16),
            pltpu.VMEM((rows_own, width), BF16),
            pltpu.VMEM((width, width), BF16),
            pltpu.VMEM((rows_own, width), BF16),
            pltpu.VMEM((rows_own, width), BF16),
            pltpu.VMEM((rows_own, width), BF16),
            pltpu.VMEM((8, 128), BF16),
            pltpu.VMEM((edge, width), F32),
            pltpu.VMEM((remote_rows, width), BF16),
            pltpu.VMEM((rows_own, width), F32),
            pltpu.SemaphoreType.DMA((5,)),
        ],
        compiler_params=pltpu.CompilerParams(vmem_limit_bytes=VMEM_LIMIT),
        name="layer",
    )(order_f, start_f, order_b, start_b, features, arrived, tile_vals, weight, cotangent)

    chips = peers // 2
    grad, weight_grad = pl.pallas_call(
        functools.partial(return_kernel, groups, locals_, slots),
        out_shape=(
            jax.ShapeDtypeStruct((rows_own, width), BF16),
            jax.ShapeDtypeStruct((width, width), F32),
        ),
        in_specs=[any_, any_, vmem, vmem],
        out_specs=(vmem, vmem),
        scratch_shapes=[
            pltpu.VMEM((remote_rows, width), BF16),
            pltpu.VMEM((rows_own, width), F32),
            pltpu.VMEM((width // 2, width), F32),
            pltpu.VMEM((width // 2, width), F32),
            pltpu.VMEM((chips, 8, width * width // 2 // chips // 8), F32),
            pltpu.VMEM((8, width * width // 2 // chips // 8), F32),
            pltpu.SemaphoreType.DMA((groups,)),
            pltpu.SemaphoreType.DMA((groups,)),
            pltpu.SemaphoreType.DMA((2,)),
            pltpu.SemaphoreType.DMA((2,)),
            pltpu.SemaphoreType.DMA((2,)),
            pltpu.SemaphoreType.DMA,
            pltpu.SemaphoreType.DMA,
            pltpu.SemaphoreType.DMA,
            pltpu.SemaphoreType.DMA,
        ],
        compiler_params=pltpu.CompilerParams(
            collective_id=1, has_side_effects=True, vmem_limit_bytes=VMEM_LIMIT
        ),
        name="give_back",
    )(remote, owned, idx.reshape(1, remote_rows), part)
    return activated, grad, weight_grad


def solution(mesh):
    groups, locals_ = mesh.shape["group"], mesh.shape["local"]
    return jax.shard_map(
        functools.partial(per_device, groups, locals_),
        mesh=mesh,
        in_specs=(
            P(("group", "local"), None),
            P(),
            P(("group", "local"), None),
            P(("group", "local"), None, None),
            P(("group", "local")),
            P(("group", "local")),
            P(("group", "local"), None, None),
            P(("group", "local"), None),
        ),
        out_specs=(P(("group", "local"), None), P(("group", "local"), None), P()),
        check_vma=False,
    )
```

time: 792 us -> 274 us (0.35)
  matrix products: 395 us -> 0 us
  Pallas kernels: 0 us -> 254 us
  waiting for transfers between devices: 215 us -> 0 us
  local copies, waits for them, and re-layouts: 79.5 us -> 9.53 us
  other arithmetic: 49.6 us -> 9.62 us
  starting transfers between devices: 20.3 us -> 0 us
  between operations: 14.7 us -> 0.71 us
  loops' own time: 12 us -> 0 us
    dot_general x51 -> x0, matrix products: 395 us -> none  [the longest x8 131 us: spread_step(): jnp.einsum('tc,tif->cif', target, product, preferred_element_type=jnp.flo...]
    pallas_call x0 -> x3, Pallas kernels: none -> 254 us  [the longest x1 109 us: per_device(): pl.pallas_call(functools.partial(return_kernel, groups, locals_, slots),...]
    all_to_all x2 -> x0, waiting for transfers between devices: 132 us -> none  [the longest x1 82.6 us: per_device(): lax.all_to_all(remote, ('group', 'local'), split_axis=0, concat_axis=0, t...]
    psum x1 -> x0, waiting for transfers between devices: 83.4 us -> none  [per_device(): weight_grad = lax.psum(partial_grad, ('group', 'local'))]
    while x34 -> x0, local copies, waits for them, and re-layouts: 37.3 us -> none
    scatter-add x1 -> x0, other arithmetic: 29.3 us -> none  [per_device(): feature_grad = owned.at[lists.reshape(-1)].add(returned.reshape(-1, width))]
    slice x3 -> x0, local copies, waits for them, and re-layouts: 20 us -> none  [the longest x2 11.8 us: per_device(): owned = spread[:rows_own]]
    all_to_all x2 -> x0, starting transfers between devices: 20 us -> none  [the longest x1 11 us: per_device(): lax.all_to_all(outgoing, ('group', 'local'), split_axis=0, concat_axis=0,...]
  transfers between devices with their start and end apart: 3 -> 0, of which waited for: 3 -> 0; matrix products, arithmetic and copies ran while one was open for 7% -> 0% of each run, Pallas kernels for 0% -> 0%
where the time goes in v1:
time: 274 us
  Pallas kernels  254 us (93%)
  other arithmetic  9.62 us (4%)
  local copies, waits for them, and re-layouts  9.53 us (3%)
    pallas_call x1, Pallas kernels, per_device(): pl.pallas_call(functools.partial(return_kernel, groups, locals_, slots),...  109 us
    pallas_call x1, Pallas kernels, per_device(): pl.pallas_call(functools.partial(exchange_kernel, groups, locals_, slots)...  81.4 us
    pallas_call x1, Pallas kernels, per_device(): pl.pallas_call(layer_kernel, out_shape=(jax.ShapeDtypeStruct((rows_own, w...  63.3 us

profile of v1, /device:TPU:39, one launch (start us, length us, event | category | flops | bytes accessed | tf_op | source)
XLA Modules:
  0.0 273.8 jit_solution(7768837554169239803)
XLA Ops:
  0.6 1.4 convert_reduce_fusion.3.start_f
  2.0 1.3 convert_reduce_fusion.2.start_b
  3.4 0.7 iota_add_fusion.1
  4.0 0.2 convert_reduce_fusion.1
  4.2 0.7 iota_add_fusion
  4.9 0.2 convert_reduce_fusion
  5.1 0.8 select_reduce_fusion.1
  5.9 0.8 select_reduce_fusion.3
  6.8 0.6 pad_add_fusion
  7.4 0.7 iota_compare_fusion.2
  8.1 0.1 lt.104
  8.2 0.8 copy.17
  9.0 0.1 squeeze.6
  9.1 0.6 broadcast_select_fusion.1.idx
  9.8 2.3 lt.105
  12.0 2.1 squeeze.7
  14.2 1.5 broadcast_select_fusion.idx
  15.7 81.4 %exchange.1.arrived = bf16[4096,512]{1,0:T(8,128)(2,1)} custom-call(bf16[2048,512]{1,0:T(8,128)(2,1)} %feat.3, s32[4096,1]{1,0:T(8,128)} %broadcast_select_fusion.idx), custom_call_target="tpu_custom_call" | custom-call | tf_op jit(solution)/shard_map/exchange/pallas_call | solution.py:377
  97.1 63.3 %layer.1 = (bf16[2048,512]{1,0:T(8,128)(2,1)}, f32[512,512]{1,0:T(8,128)}, bf16[4096,512]{1,0:T(8,128)(2,1)}, f32[2048,512]{1,0:T(8,128)}) custom-call(s32[512]{0:T(512)} %get-tuple-element.19.order_f, s32[17]{0:T(128)} %convert_reduce_fusion.3.start_f, s32[512]{0:T(512)} %get-tuple-element.20.order_b, s32[49]{0:T(128)} %convert_reduce_fusion.2.start_b, ...), custom_call_target="tpu_custom_call" | custom-call | tf_op jit(solution)/shard_map/layer/pallas_call | solution.py:394
  160.4 109.3 %give_back.1 = (bf16[2048,512]{1,0:T(8,128)(2,1)}, f32[512,512]{1,0:T(8,128)}) custom-call(bf16[4096,512]{1,0:T(8,128)(2,1)} %get-tuple-element.10.remote, f32[2048,512]{1,0:T(8,128)} %get-tuple-element.11.owned, s32[1,4096]{1,0:T(1,128)} %broadcast_select_fusion.1.idx, f32[512,512]{1,0:T(8,128)} %get-tuple-element.12.part), custom_call_target="tpu_custom_call" | custom-call | tf_op jit(solution)/shard_map/give_back/pallas_call | solution.py:423
  269.7 0.0 copy-start
  269.7 3.1 %copy.23 = bf16[2048,512]{1,0:T(8,128)(2,1)} copy(bf16[2048,512]{1,0:T(8,128)(2,1)} %get-tuple-element.25) | data formatting | bytes 4194304
  272.8 0.0 copy-done
  272.8 1.0 copy.24
Async XLA Ops:
  269.7 3.1 %copy-start = (f32[512,512]{1,0:T(8,128)S(1)}, f32[512,512]{1,0:T(8,128)}, u32[]{:S(2)}) copy-start(f32[512,512]{1,0:T(8,128)} %get-tuple-element.26) | copy-start | bytes 3145732

commit v2 on v0

v2 whole, which is shorter than its diff:
```python
import functools

import jax
import jax.numpy as jnp
from jax import lax
from jax.experimental import pallas as pl
from jax.experimental.pallas import tpu as pltpu
from jax.sharding import PartitionSpec as P

MESH = pl.DeviceIdType.MESH
F32 = jnp.float32
BF16 = jnp.bfloat16
VMEM_LIMIT = 60 * 1024 * 1024
EDGE = 128
SIDE = 4
SQUARE = 8
SQUARES = SIDE * SIDE
DEVICES = SQUARES * SQUARE
BATCHES = SQUARES // 2
PEERS = 2 * SQUARE


def span(at, size):
    return pl.ds(pl.multiple_of(at, size), size)


def wait_rows(ref, rows, sem):
    view = ref.at[pl.ds(0, rows)]
    pltpu.make_async_copy(view, view, sem).wait()


def network_kernel(
    cells, earlier,
    lists, live, feat_in, vals, weight_in, cot_in,
    activated, grad, wgrad,
    feat, tiles, rest, flipped, wbuf, cot, lst, rowtab, outgoing, arrived, acc, hid,
    returned, block, part, wsum, sib, chunks, gathered,
    load_sem, save_sem, send1, recv1, send2, recv2, sib_send, sib_recv, rs_send, rs_recv, ag_send, ag_recv,
):
    me = lax.axis_index("group") * (2 * SQUARE) + lax.axis_index("local")
    z, x = me // (SIDE * SQUARE), (me // SQUARE) % SIDE
    y, core = (me // 2) % SIDE, me % 2
    my_slot = y * 2 + core
    count = vals.shape[0]
    rows_own, width = feat.shape
    slots = lists.shape[1]
    row_blocks = rows_own // EDGE
    cols_all = row_blocks + DEVICES * slots // EDGE
    half_batch = SQUARE * slots
    batch = 2 * half_batch
    wide = batch // EDGE

    def device(square, slot):
        return (square // 2, (square % 2) * SQUARE + slot)

    def square_of(k, a, sign):
        dz, dx = k // SIDE + 2 * a, k % SIDE + 2 * a
        return ((z + SIDE + sign * dz) % SIDE) * SIDE + (x + 2 * SIDE + sign * dx) % SIDE

    loads = [
        pltpu.make_async_copy(feat_in, feat, load_sem.at[0]),
        pltpu.make_async_copy(vals, tiles.at[pl.ds(0, count)], load_sem.at[1]),
        pltpu.make_async_copy(cot_in, cot, load_sem.at[2]),
        pltpu.make_async_copy(weight_in, wbuf, load_sem.at[3]),
    ]
    for load in loads:
        load.start()

    barrier = pltpu.get_barrier_semaphore()

    @pl.loop(1, DEVICES)
    def _(k):
        peer = (me + k) % DEVICES
        pl.semaphore_signal(
            barrier, inc=1, device_id=device(peer // SQUARE, peer % SQUARE), device_id_type=MESH
        )

    lst[...] = jnp.full(lst.shape, -1, jnp.int32)
    limit = jnp.broadcast_to(live[...], (DEVICES, DEVICES)).T[:, :slots]
    lst[:, :slots] = jnp.where(
        lax.broadcasted_iota(jnp.int32, (DEVICES, slots), 1) < limit, lists[...], -1
    )

    def gather(k):
        picks = []
        for a in (0, 1):
            columns = lst[span(square_of(k, a, 1) * SQUARE, SQUARE), :].T
            picks += [columns[:slots, j : j + 1] for j in range(SQUARE)]
        ids = lax.broadcasted_iota(jnp.int32, (slots, rows_own), 1)
        onehot = jnp.concatenate([(pick == ids).astype(F32).astype(BF16) for pick in picks], axis=0)
        outgoing[span(k * batch, batch), :] = jnp.dot(
            onehot, feat[...], preferred_element_type=F32
        ).astype(BF16)

    def send(k, i, landing, send_sem, recv_sem):
        a, dy, dc = i % 2, (2 + i // 2) % SIDE, i // SQUARE
        slot = ((y + dy) % SIDE) * 2 + (core + dc) % 2
        base = k * batch + a * half_batch
        pltpu.make_async_remote_copy(
            src_ref=outgoing.at[span(base + slot * slots, slots)],
            dst_ref=landing.at[span(base + my_slot * slots, slots)],
            send_sem=send_sem.at[k],
            recv_sem=recv_sem.at[k],
            device_id=device(square_of(k, a, 1), slot),
            device_id_type=MESH,
        ).start()

    def send_first(landing, send_sem, recv_sem):
        for i in range(PEERS):
            if i != 4:
                send(0, i, landing, send_sem, recv_sem)
        mine = span(my_slot * slots, slots)
        landing[mine, :] = outgoing[mine, :]

    def send_batch(k, landing, send_sem, recv_sem):
        @pl.loop(0, PEERS)
        def _(i):
            send(k, i, landing, send_sem, recv_sem)

    loads[0].wait()
    gather(0)
    pl.semaphore_wait(barrier, DEVICES - 1)
    send_first(arrived, send1, recv1)

    @pl.loop(1, BATCHES)
    def _(k):
        gather(k)
        send_batch(k, arrived, send1, recv1)

    for empty in (tiles, rest, flipped):
        empty[count] = jnp.zeros((EDGE, EDGE), BF16)
    loads[1].wait()

    @pl.loop(0, count)
    def _(t):
        before = earlier[t]
        exact = tiles[t].astype(F32) + (tiles[before].astype(F32) + rest[before].astype(F32))
        merged = exact.astype(BF16)
        rest[t] = (exact - merged.astype(F32)).astype(BF16)
        tiles[t] = merged
        flipped[t] = merged.T

    lane = lax.broadcasted_iota(jnp.int32, (SQUARES, EDGE), 1) // slots
    per = EDGE // slots
    for h in range(SQUARE // per):
        line = jnp.full((SQUARES, EDGE), -1, jnp.int32)
        for j in range(per):
            row = lst[pl.ds(h * per + j, SQUARES, stride=SQUARE), :]
            line = jnp.where(lane == j, pltpu.roll(row, j * slots, 1) if j else row, line)
        rowtab[:, h * EDGE : (h + 1) * EDGE] = line

    def remote_cols(k, sign):
        per_square = half_batch // EDGE
        first = [row_blocks + square_of(k, a, sign) * per_square for a in (0, 1)]
        return [f + n for f in first for n in range(per_square)]

    def forward(cols, source, fresh):
        @pl.loop(0, row_blocks // wide)
        def _(m):
            left = jnp.concatenate(
                [
                    jnp.concatenate([tiles[cells[(m * wide + r) * cols_all + c]] for c in cols], axis=1)
                    for r in range(wide)
                ],
                axis=0,
            )
            product = jnp.dot(left, source, preferred_element_type=F32)
            at = span(m * batch, batch)
            if fresh:
                acc[at, :] = product
            else:
                acc[at, :] += product

    def own_cols(n):
        return [n * wide + j for j in range(wide)]

    forward(own_cols(0), feat[span(0, batch), :], True)

    @pl.loop(1, row_blocks // wide)
    def _(n):
        forward(own_cols(n), feat[span(n * batch, batch), :], False)

    def take_batch(k):
        forward(remote_cols(k, -1), arrived[span(k * batch, batch), :], False)

    wait_rows(arrived, batch - slots, recv1.at[0])
    take_batch(0)

    @pl.loop(1, BATCHES)
    def _(k):
        wait_rows(arrived, batch, recv1.at[k])
        take_batch(k)

    loads[2].wait()
    loads[3].wait()

    slope, hgrad = arrived.at[pl.ds(0, rows_own)], arrived.at[pl.ds(rows_own, rows_own)]

    @pl.loop(0, rows_own // batch)
    def _(b):
        at = span(b * batch, batch)
        h = acc[at, :].astype(BF16)
        hid[at, :] = h
        pre = jnp.dot(h, wbuf[...], preferred_element_type=F32)
        gate = jax.nn.sigmoid(pre)
        s = (cot[at, :].astype(F32) * gate * (1.0 + pre * (1.0 - gate))).astype(BF16)
        cot[at, :] = (pre * gate).astype(BF16)
        slope[at, :] = s
        hgrad[at, :] = lax.dot_general(
            s, wbuf[...], (((1,), (1,)), ((), ())), preferred_element_type=F32
        ).astype(BF16)

    save_act = pltpu.make_async_copy(cot, activated, save_sem)
    save_act.start()

    def spread(cols):
        block[...] = jnp.zeros_like(block)

        @pl.loop(0, row_blocks // wide)
        def _(m):
            left = jnp.concatenate(
                [
                    jnp.concatenate([flipped[cells[(m * wide + r) * cols_all + c]] for r in range(wide)], axis=1)
                    for c in cols
                ],
                axis=0,
            )
            block[...] += jnp.dot(left, hgrad[span(m * batch, batch), :], preferred_element_type=F32)

    def give(k):
        spread(remote_cols(k, 1))
        outgoing[span(k * batch, batch), :] = block[...].astype(BF16)

    wait_rows(outgoing, batch - slots, send1.at[0])
    give(0)
    send_first(returned, send2, recv2)

    part[...] = jnp.zeros_like(part)

    @pl.loop(0, rows_own // batch)
    def _(b):
        at = span(b * batch, batch)
        part[...] += lax.dot_general(
            hid[at, :], slope[at, :], (((0,), (0,)), ((), ())), preferred_element_type=F32
        )

    half = width // 2
    mine, other = pl.multiple_of(core * half, half), pl.multiple_of((1 - core) * half, half)
    chips = DEVICES // 2
    chip = me // 2
    square = me // SQUARE
    edge_r, edge_c = chunks.shape[1:]
    across = width // edge_c
    sibling = device(square, y * 2 + 1 - core)
    swap = pltpu.make_async_remote_copy(
        src_ref=part.at[pl.ds(other, half)],
        dst_ref=sib,
        send_sem=sib_send.at[0],
        recv_sem=sib_recv.at[0],
        device_id=sibling,
        device_id_type=MESH,
    )
    swap.start()

    wait_rows(outgoing, batch, send1.at[1])
    give(1)
    send_batch(1, returned, send2, recv2)
    swap.wait()
    wsum[...] = part[pl.ds(mine, half), :] + sib[...]

    def spot(q):
        return q // across * edge_r, q % across * edge_c

    def mate(q):
        return device(q // SIDE, q % SIDE * 2 + core)

    @pl.loop(1, chips)
    def _(k):
        q = (chip + k) % chips
        r0, c0 = spot(q)
        pltpu.make_async_remote_copy(
            src_ref=wsum.at[span(r0, edge_r), span(c0, edge_c)],
            dst_ref=chunks.at[chip],
            send_sem=rs_send,
            recv_sem=rs_recv,
            device_id=mate(q),
            device_id_type=MESH,
        ).start()

    r0, c0 = spot(chip)
    chunks[chip] = wsum[span(r0, edge_r), span(c0, edge_c)]

    @pl.loop(2, BATCHES)
    def _(k):
        wait_rows(outgoing, batch, send1.at[k])
        give(k)
        send_batch(k, returned, send2, recv2)

    wait_rows(chunks, chips - 1, rs_send)
    wait_rows(chunks, chips - 1, rs_recv)
    gathered[...] = jnp.sum(chunks[...], axis=0)
    there = (span(mine + r0, edge_r), span(c0, edge_c))
    wgrad[there[0], there[1]] = gathered[...]

    @pl.loop(1, chips)
    def _(k):
        pltpu.make_async_remote_copy(
            src_ref=gathered,
            dst_ref=wgrad.at[there[0], there[1]],
            send_sem=ag_send,
            recv_sem=ag_recv,
            device_id=mate((chip + k) % chips),
            device_id_type=MESH,
        ).start()

    @pl.loop(0, row_blocks // wide)
    def _(n):
        spread(own_cols(n))
        acc[span(n * batch, batch), :] = block[...]

    def add_batch(k):
        picks = jnp.concatenate([rowtab[pl.ds(square_of(k, a, -1), 1), :] for a in (0, 1)], axis=1)
        rows = returned[span(k * batch, batch), :]

        @pl.loop(0, rows_own // 1024)
        def _(b):
            ids = lax.broadcasted_iota(jnp.int32, (1024, batch), 0) + b * 1024
            onehot = (ids == picks).astype(F32).astype(BF16)
            acc[span(b * 1024, 1024), :] += jnp.dot(onehot, rows, preferred_element_type=F32)

    wait_rows(returned, batch - slots, recv2.at[0])
    add_batch(0)

    @pl.loop(1, BATCHES)
    def _(k):
        wait_rows(returned, batch, recv2.at[k])
        add_batch(k)

    wait_rows(chunks, chips - 1, ag_send)
    wait_rows(chunks, chips - 1, ag_recv)
    back = pltpu.make_async_remote_copy(
        src_ref=wgrad.at[pl.ds(mine, half)],
        dst_ref=wgrad.at[pl.ds(mine, half)],
        send_sem=sib_send.at[1],
        recv_sem=sib_recv.at[1],
        device_id=sibling,
        device_id_type=MESH,
    )
    back.start()
    grad[...] = acc[...].astype(BF16)
    wait_rows(returned, batch - slots, send2.at[0])

    @pl.loop(1, BATCHES)
    def _(k):
        wait_rows(returned, batch, send2.at[k])

    save_act.wait()
    back.wait()


def per_device(features, weight, cotangent, tile_vals, tile_rows, tile_cols, send_rows, counts):
    rows_own, width = features.shape
    count = tile_vals.shape[0]
    slots = send_rows.shape[2]
    row_blocks = rows_own // EDGE
    remote_rows = DEVICES * slots
    cols_all = row_blocks + remote_rows // EDGE
    batch = 2 * SQUARE * slots

    ids = jnp.arange(count, dtype=jnp.int32)
    cell = tile_rows * cols_all + tile_cols
    same = (cell[None, :] == cell[:, None]) & (ids[None, :] < ids[:, None])
    earlier = jnp.max(jnp.where(same, ids[None, :], -1), axis=1)
    earlier = jnp.where(earlier < 0, count, earlier)
    there = cell[None, :] == jnp.arange(row_blocks * cols_all, dtype=jnp.int32)[:, None]
    cells = jnp.max(jnp.where(there, ids[None, :], -1), axis=1)
    cells = jnp.where(cells < 0, count, cells)

    any_ = pl.BlockSpec(memory_space=pl.ANY)
    vmem = pl.BlockSpec(memory_space=pltpu.VMEM)
    smem = pl.BlockSpec(memory_space=pltpu.SMEM)
    chips = DEVICES // 2
    edge_c = width * width // 2 // chips // 8
    dma = pltpu.SemaphoreType.DMA
    rows16 = pltpu.VMEM((rows_own, width), BF16)
    far16 = pltpu.VMEM((remote_rows, width), BF16)
    activated, grad, weight_grad = pl.pallas_call(
        network_kernel,
        out_shape=(
            jax.ShapeDtypeStruct((rows_own, width), BF16),
            jax.ShapeDtypeStruct((rows_own, width), BF16),
            jax.ShapeDtypeStruct((width, width), F32),
        ),
        in_specs=[smem, smem, vmem, vmem] + [any_] * 4,
        out_specs=(any_, vmem, vmem),
        scratch_shapes=[
            rows16,
            pltpu.VMEM((count + 1, EDGE, EDGE), BF16),
            pltpu.VMEM((count + 1, EDGE, EDGE), BF16),
            pltpu.VMEM((count + 1, EDGE, EDGE), BF16),
            pltpu.VMEM((width, width), BF16),
            rows16,
            pltpu.VMEM((DEVICES, EDGE), jnp.int32),
            pltpu.VMEM((SQUARES, SQUARE * slots), jnp.int32),
            far16,
            far16,
            pltpu.VMEM((rows_own, width), F32),
            rows16,
            far16,
            pltpu.VMEM((batch, width), F32),
            pltpu.VMEM((width, width), F32),
            pltpu.VMEM((width // 2, width), F32),
            pltpu.VMEM((width // 2, width), F32),
            pltpu.VMEM((chips, 8, edge_c), F32),
            pltpu.VMEM((8, edge_c), F32),
            dma((4,)),
            dma,
            dma((BATCHES,)),
            dma((BATCHES,)),
            dma((BATCHES,)),
            dma((BATCHES,)),
            dma((2,)),
            dma((2,)),
            dma,
            dma,
            dma,
            dma,
        ],
        compiler_params=pltpu.CompilerParams(
            collective_id=0, has_side_effects=True, vmem_limit_bytes=VMEM_LIMIT
        ),
        name="network",
    )(cells, earlier, send_rows[0], counts, features, tile_vals, weight, cotangent)
    return activated, grad, weight_grad


def solution(mesh):
    rows = P(("group", "local"), None)
    tiles = P(("group", "local"), None, None)
    flat = P(("group", "local"))
    return jax.shard_map(
        per_device,
        mesh=mesh,
        in_specs=(rows, P(), rows, tiles, flat, flat, tiles, rows),
        out_specs=(rows, rows, P()),
        check_vma=False,
    )
```

time: 792 us -> 157 us (0.20)
  matrix products: 395 us -> 0 us
  waiting for transfers between devices: 215 us -> 0 us
  Pallas kernels: 0 us -> 145 us
  local copies, waits for them, and re-layouts: 79.5 us -> 7.57 us
  other arithmetic: 49.6 us -> 2.23 us
  starting transfers between devices: 20.3 us -> 0 us
  between operations: 14.7 us -> 0.66 us
  loops' own time: 12 us -> 0 us
    dot_general x51 -> x0, matrix products: 395 us -> none  [the longest x8 131 us: spread_step(): jnp.einsum('tc,tif->cif', target, product, preferred_element_type=jnp.flo...]
    pallas_call x0 -> x1, Pallas kernels: none -> 145 us  [per_device(): pl.pallas_call(network_kernel, out_shape=(jax.ShapeDtypeStruct((rows_own,...]
    all_to_all x2 -> x0, waiting for transfers between devices: 132 us -> none  [the longest x1 82.6 us: per_device(): lax.all_to_all(remote, ('group', 'local'), split_axis=0, concat_axis=0, t...]
    psum x1 -> x0, waiting for transfers between devices: 83.4 us -> none  [per_device(): weight_grad = lax.psum(partial_grad, ('group', 'local'))]
    while x34 -> x0, local copies, waits for them, and re-layouts: 37.3 us -> none
    scatter-add x1 -> x0, other arithmetic: 29.3 us -> none  [per_device(): feature_grad = owned.at[lists.reshape(-1)].add(returned.reshape(-1, width))]
    slice x3 -> x0, local copies, waits for them, and re-layouts: 20 us -> none  [the longest x2 11.8 us: per_device(): owned = spread[:rows_own]]
    all_to_all x2 -> x0, starting transfers between devices: 20 us -> none  [the longest x1 11 us: per_device(): lax.all_to_all(outgoing, ('group', 'local'), split_axis=0, concat_axis=0,...]
  transfers between devices with their start and end apart: 3 -> 0, of which waited for: 3 -> 0; matrix products, arithmetic and copies ran while one was open for 7% -> 0% of each run, Pallas kernels for 0% -> 0%
where the time goes in v2:
time: 157 us; the launch traced here: 156 us
  Pallas kernels  145 us (92%)
  local copies, waits for them, and re-layouts  7.57 us (5%)
  other arithmetic  2.23 us (1%)
    pallas_call x1, Pallas kernels, per_device(): pl.pallas_call(network_kernel, out_shape=(jax.ShapeDtypeStruct((rows_own,...  145 us
    unnamed x8, local copies, waits for them, and re-layouts  7.57 us

profile of v2, /device:TPU:39, one launch (start us, length us, event | category | flops | bytes accessed | tf_op | source)
XLA Modules:
  0.0 155.6 jit_solution(1822245244628417188)
XLA Ops:
  0.6 0.7 multiply_add_fusion
  1.3 0.2 select_reduce_fusion.1
  1.5 0.6 compare_select_fusion.1.earlier
  2.1 0.2 select_reduce_fusion
  2.3 0.6 compare_select_fusion.cells
  2.9 1.4 copy.12
  4.3 145.1 %network.1 = (bf16[2048,512]{1,0:T(8,128)(2,1)}, bf16[2048,512]{1,0:T(8,128)(2,1)}, f32[512,512]{1,0:T(8,128)}) custom-call(s32[768]{0:T(1024)} %compare_select_fusion.cells, s32[256]{0:T(256)} %compare_select_fusion.1.earlier, s32[128,32]{1,0:T(8,128)} %bitcast.1, s32[1,128]{1,0:T(1,128)} %live.1, bf16[2048,512]{1,0:T(8,128)(2,1)} %feat_in.1, ...), custom_call_target="tpu_custom_call" | custom-call | tf_op jit(solution)/shard_map/network/pallas_call | solution.py:387
  149.5 0.0 copy-start
  149.5 3.2 %copy.16 = bf16[2048,512]{1,0:T(8,128)(2,1)} copy(bf16[2048,512]{1,0:T(8,128)(2,1)} %get-tuple-element.6) | data formatting | bytes 4194304
  152.7 0.0 copy-done
  152.7 0.0 copy-start.1
  152.7 1.3 copy.17
  154.0 0.6 copy-done.1
  154.6 1.0 copy.18
Async XLA Ops:
  149.5 3.2 %copy-start = (bf16[2048,512]{1,0:T(8,128)(2,1)S(1)}, bf16[2048,512]{1,0:T(8,128)(2,1)}, u32[]{:S(2)}) copy-start(bf16[2048,512]{1,0:T(8,128)(2,1)} %get-tuple-element.7) | copy-start | bytes 6291460
  152.7 2.0 %copy-start.1 = (f32[512,512]{1,0:T(8,128)S(1)}, f32[512,512]{1,0:T(8,128)}, u32[]{:S(2)}) copy-start(f32[512,512]{1,0:T(8,128)} %get-tuple-element.8) | copy-start | bytes 3145732

commit v3 on v2

v3 whole, which is shorter than its diff:
```python
import functools

import jax
import jax.numpy as jnp
from jax import lax
from jax.experimental import pallas as pl
from jax.experimental.pallas import tpu as pltpu
from jax.sharding import PartitionSpec as P

MESH = pl.DeviceIdType.MESH
F32 = jnp.float32
BF16 = jnp.bfloat16
VMEM_LIMIT = 60 * 1024 * 1024
EDGE = 128
SIDE = 4
SQUARE = 8
SQUARES = SIDE * SIDE
DEVICES = SQUARES * SQUARE
BATCHES = SQUARES // 2
PARTS = 4


def div(a, b):
    return a // b if isinstance(a, int) else lax.div(a, b)


def rem(a, b):
    return a % b if isinstance(a, int) else lax.rem(a, b)


def span(at, size):
    return pl.ds(pl.multiple_of(at, size), size)


def wait_rows(ref, rows, sem):
    view = ref.at[pl.ds(0, rows)]
    pltpu.make_async_copy(view, view, sem).wait()


def network_kernel(
    lists, live, tile_rows, tile_cols, feat_in, vals, weight_in, cot_in,
    activated, grad, wgrad,
    plan_v, plan, feat, tiles, rest, flipped, wbuf, cot, lst, rowtab, outgoing, arrived, acc, hid, slope, hgrad,
    returned, part, wsum, sib, chunks, gathered, wall,
    load_sem, save_sem, send1, recv1, send2, recv2, sib_send, sib_recv, rs_send, rs_recv, ag_send, ag_recv,
):
    me = lax.axis_index("group") * (2 * SQUARE) + lax.axis_index("local")
    z, x = div(me, SIDE * SQUARE), rem(div(me, SQUARE), SIDE)
    y, core = rem(div(me, 2), SIDE), rem(me, 2)
    my_slot = y * 2 + core
    count = vals.shape[0]
    rows_own, width = feat.shape
    slots = lists.shape[0]
    row_blocks = rows_own // EDGE
    cols_all = row_blocks + DEVICES * slots // EDGE
    half_batch = SQUARE * slots
    batch = 2 * half_batch
    wide = batch // EDGE

    def device(square, slot):
        return (div(square, 2), rem(square, 2) * SQUARE + slot)

    def square_of(k, a, sign):
        dz, dx = div(k, SIDE) + 2 * a, rem(k, SIDE) + 2 * a
        return rem(z + SIDE + sign * dz, SIDE) * SIDE + rem(x + 2 * SIDE + sign * dx, SIDE)

    loads = [
        pltpu.make_async_copy(feat_in, feat, load_sem.at[0]),
        pltpu.make_async_copy(vals, tiles.at[pl.ds(0, count)], load_sem.at[1]),
        pltpu.make_async_copy(cot_in, cot, load_sem.at[2]),
        pltpu.make_async_copy(weight_in, wbuf, load_sem.at[3]),
    ]
    for load in loads:
        load.start()

    barrier = pltpu.get_barrier_semaphore()

    def greet(square, slot):
        pl.semaphore_signal(barrier, inc=1, device_id=device(square, slot), device_id_type=MESH)

    my_square = div(me, SQUARE)
    for j in range(1, SQUARE):
        greet(my_square, rem(my_slot + j, SQUARE))

    @pl.loop(1, SQUARES)
    def _(k):
        square = rem(my_square + k, SQUARES)
        for j in range(SQUARE):
            greet(square, j)

    rank = lax.broadcasted_iota(jnp.int32, (slots, DEVICES), 0)
    masked = jnp.where(rank < live[...], lists[...], -1)
    lst[...] = jnp.concatenate([masked, jnp.full((EDGE - slots, DEVICES), -1, jnp.int32)], axis=0).T

    def gather(k):
        picks = []
        for a in (0, 1):
            columns = lst[span(square_of(k, a, 1) * SQUARE, SQUARE), :].T
            picks += [columns[:slots, j : j + 1] for j in range(SQUARE)]
        ids = lax.broadcasted_iota(jnp.int32, (slots, rows_own), 1)
        onehot = jnp.concatenate([(pick == ids).astype(F32).astype(BF16) for pick in picks], axis=0)
        outgoing[span(k * batch, batch), :] = jnp.dot(
            onehot, feat[...], preferred_element_type=F32
        ).astype(BF16)

    slot_at = {
        (dy, dc): rem(y + dy, SIDE) * 2 + rem(core + dc, 2) for dy in range(SIDE) for dc in range(2)
    }

    def send_batch(k, landing, send_sem, recv_sem, with_self=False):
        squares = [square_of(k, a, 1) for a in (0, 1)]
        bases = [pl.multiple_of(k * batch + a * half_batch, half_batch) for a in (0, 1)]
        for dc in (0, 1):
            for dy in (2, 3, 0, 1):
                for a in (0, 1):
                    if with_self and (a, dy, dc) == (0, 0, 0):
                        continue
                    slot = slot_at[dy, dc]
                    pltpu.make_async_remote_copy(
                        src_ref=outgoing.at[span(bases[a] + slot * slots, slots)],
                        dst_ref=landing.at[span(bases[a] + my_slot * slots, slots)],
                        send_sem=send_sem.at[k],
                        recv_sem=recv_sem.at[k],
                        device_id=device(squares[a], slot),
                        device_id_type=MESH,
                    ).start()

    def send_first(landing, send_sem, recv_sem):
        send_batch(0, landing, send_sem, recv_sem, True)
        mine = span(my_slot * slots, slots)
        landing[mine, :] = outgoing[mine, :]

    loads[0].wait()
    gather(0)
    pl.semaphore_wait(barrier, DEVICES - 1)
    send_first(arrived, send1, recv1)

    @pl.loop(1, BATCHES)
    def _(k):
        gather(k)
        send_batch(k, arrived, send1, recv1)

    keys = tile_rows[...] * cols_all + tile_cols[...]
    column = jnp.broadcast_to(keys, (EDGE, count)).T
    tile_ids = lax.broadcasted_iota(jnp.int32, (count, EDGE), 0)
    lanes = lax.broadcasted_iota(jnp.int32, (1, EDGE), 1)

    def last_of(hit):
        found = jnp.max(jnp.where(hit, tile_ids, -1), axis=0, keepdims=True)
        return jnp.where(found < 0, count, found)

    for r in range(row_blocks):
        plan_v[r : r + 1, :] = last_of((column == r * cols_all + lanes) & (lanes < cols_all))
    for h in range(count // EDGE):
        own = keys[:, h * EDGE : (h + 1) * EDGE]
        plan_v[row_blocks + h : row_blocks + h + 1, :] = last_of(
            (column == own) & (tile_ids < lanes + h * EDGE)
        )
    save_plan = pltpu.make_async_copy(plan_v, plan, save_sem)
    save_plan.start()
    save_plan.wait()

    for empty in (tiles, rest, flipped):
        empty[count] = jnp.zeros((EDGE, EDGE), BF16)
    loads[1].wait()

    unroll = 4
    for h in range(count // EDGE):

        @pl.loop(0, EDGE // unroll)
        def _(i):
            for u in range(unroll):
                t = h * EDGE + i * unroll + u
                before = plan[row_blocks + h, i * unroll + u]
                exact = tiles[t].astype(F32) + (tiles[before].astype(F32) + rest[before].astype(F32))
                merged = exact.astype(BF16)
                rest[t] = (exact - merged.astype(F32)).astype(BF16)
                tiles[t] = merged

    @pl.loop(0, count // 8)
    def _(i):
        for u in range(8):
            flipped[i * 8 + u] = tiles[i * 8 + u].T

    lane = lax.broadcasted_iota(jnp.int32, (SQUARES, EDGE), 1) // slots
    per = EDGE // slots
    for h in range(SQUARE // per):
        line = jnp.full((SQUARES, EDGE), -1, jnp.int32)
        for j in range(per):
            row = lst[pl.ds(h * per + j, SQUARES, stride=SQUARE), :]
            line = jnp.where(lane == j, pltpu.roll(row, j * slots, 1) if j else row, line)
        rowtab[:, h * EDGE : (h + 1) * EDGE] = line

    def remote_cols(k, sign):
        per_square = half_batch // EDGE
        first = [row_blocks + square_of(k, a, sign) * per_square for a in (0, 1)]
        return [f + n for f in first for n in range(per_square)]

    def left_of(cols, m):
        bands = [
            jnp.concatenate([tiles[plan[m * wide + r, c]] for c in cols], axis=1) for r in range(wide)
        ]
        return jnp.concatenate(bands, axis=0)

    @pl.loop(0, row_blocks // wide)
    def _(m):
        acc[span(m * batch, batch), :] = jnp.dot(
            left_of(range(row_blocks), m), feat[...], preferred_element_type=F32
        )

    def take(cols, source):
        @pl.loop(0, row_blocks // wide)
        def _(m):
            acc[span(m * batch, batch), :] += jnp.dot(left_of(cols, m), source, preferred_element_type=F32)

    wait_rows(arrived, batch - slots, recv1.at[0])
    take(remote_cols(0, -1), arrived[span(0, batch), :])

    @pl.loop(0, (BATCHES - 2) // 2)
    def _(i):
        k = 1 + 2 * i
        for n in (0, 1):
            wait_rows(arrived, batch, recv1.at[k + n])
        take(remote_cols(k, -1) + remote_cols(k + 1, -1), arrived[pl.ds(pl.multiple_of(k * batch, batch), 2 * batch), :])

    loads[2].wait()
    loads[3].wait()
    last = BATCHES - 1
    wait_rows(arrived, batch, recv1.at[last])
    cols = remote_cols(last, -1)
    source = arrived[span(last * batch, batch), :]
    for b in range(rows_own // batch):
        at = pl.ds(b * batch, batch)
        h = (acc[at, :] + jnp.dot(left_of(cols, b), source, preferred_element_type=F32)).astype(BF16)
        hid[at, :] = h
        pre = jnp.dot(h, wbuf[...], preferred_element_type=F32)
        gate = jax.nn.sigmoid(pre)
        s = (cot[at, :].astype(F32) * gate * (1.0 + pre * (1.0 - gate))).astype(BF16)
        cot[at, :] = (pre * gate).astype(BF16)
        slope[at, :] = s
        hgrad[at, :] = lax.dot_general(
            s, wbuf[...], (((1,), (1,)), ((), ())), preferred_element_type=F32
        ).astype(BF16)

    save_act = pltpu.make_async_copy(cot, activated, save_sem)
    save_act.start()

    def spread(cols):
        bands = [
            jnp.concatenate([flipped[plan[r, c]] for r in range(row_blocks)], axis=1) for c in cols
        ]
        return jnp.dot(jnp.concatenate(bands, axis=0), hgrad[...], preferred_element_type=F32)

    def give(k):
        outgoing[span(k * batch, batch), :] = spread(remote_cols(k, 1)).astype(BF16)

    wait_rows(outgoing, batch - slots, send1.at[0])
    give(0)
    send_first(returned, send2, recv2)

    part[...] = jnp.zeros_like(part)

    @pl.loop(0, rows_own // batch)
    def _(b):
        at = span(b * batch, batch)
        part[...] += lax.dot_general(
            hid[at, :], slope[at, :], (((0,), (0,)), ((), ())), preferred_element_type=F32
        )

    half = width // 2
    mine, other = pl.multiple_of(core * half, half), pl.multiple_of((1 - core) * half, half)
    chips = DEVICES // 2
    chip = div(me, 2)
    square = div(me, SQUARE)
    edge_r, edge_c = chunks.shape[1:]
    across = width // edge_c
    sibling = device(square, y * 2 + 1 - core)
    swap = pltpu.make_async_remote_copy(
        src_ref=part.at[pl.ds(other, half)],
        dst_ref=sib,
        send_sem=sib_send.at[0],
        recv_sem=sib_recv.at[0],
        device_id=sibling,
        device_id_type=MESH,
    )
    swap.start()

    wait_rows(outgoing, batch, send1.at[1])
    give(1)
    send_batch(1, returned, send2, recv2)
    swap.wait()
    wsum[...] = (part[pl.ds(mine, half), :] + sib[...]).astype(BF16)

    def spot(q):
        return div(q, across) * edge_r, rem(q, across) * edge_c

    def mate(q):
        return device(div(q, SIDE), rem(q, SIDE) * 2 + core)

    @pl.loop(1, chips)
    def _(k):
        q = rem(chip + k, chips)
        r0, c0 = spot(q)
        pltpu.make_async_remote_copy(
            src_ref=wsum.at[span(r0, edge_r), span(c0, edge_c)],
            dst_ref=chunks.at[chip],
            send_sem=rs_send,
            recv_sem=rs_recv,
            device_id=mate(q),
            device_id_type=MESH,
        ).start()

    r0, c0 = spot(chip)
    chunks[chip] = wsum[span(r0, edge_r), span(c0, edge_c)]

    def give_batch(k):
        wait_rows(outgoing, batch, send1.at[k])
        give(k)
        send_batch(k, returned, send2, recv2)

    @pl.loop(2, BATCHES // 2)
    def _(k):
        give_batch(k)

    @pl.loop(0, row_blocks // wide)
    def _(n):
        acc[span(n * batch, batch), :] = spread([n * wide + j for j in range(wide)])

    wait_rows(chunks, chips - 1, rs_send)
    wait_rows(chunks, chips - 1, rs_recv)
    gathered[...] = jnp.sum(chunks[...].astype(F32), axis=0).astype(BF16)
    there = (span(mine + r0, edge_r), span(c0, edge_c))
    wall[there[0], there[1]] = gathered[...]

    @pl.loop(1, chips)
    def _(k):
        pltpu.make_async_remote_copy(
            src_ref=gathered,
            dst_ref=wall.at[there[0], there[1]],
            send_sem=ag_send,
            recv_sem=ag_recv,
            device_id=mate(rem(chip + k, chips)),
            device_id_type=MESH,
        ).start()

    @pl.loop(BATCHES // 2, BATCHES)
    def _(k):
        give_batch(k)

    tall = 1024

    def picks_of(k):
        return jnp.concatenate([rowtab[pl.ds(square_of(k, a, -1), 1), :] for a in (0, 1)], axis=1)

    def hits(picks, rows, b):
        ids = lax.broadcasted_iota(jnp.int32, (tall, batch), 0) + b * tall
        onehot = (ids == picks).astype(F32).astype(BF16)
        return jnp.dot(onehot, rows, preferred_element_type=F32)

    def add_batch(k):
        picks, rows = picks_of(k), returned[span(k * batch, batch), :]

        @pl.loop(0, rows_own // tall)
        def _(b):
            acc[span(b * tall, tall), :] += hits(picks, rows, b)

    def take_back(k):
        wait_rows(returned, batch, recv2.at[k])
        add_batch(k)

    wait_rows(returned, batch - slots, recv2.at[0])
    add_batch(0)

    @pl.loop(1, BATCHES // 2 + 1)
    def _(k):
        take_back(k)

    wait_rows(chunks, chips - 1, ag_send)
    wait_rows(chunks, chips - 1, ag_recv)
    back = pltpu.make_async_remote_copy(
        src_ref=wall.at[pl.ds(mine, half)],
        dst_ref=wall.at[pl.ds(mine, half)],
        send_sem=sib_send.at[1],
        recv_sem=sib_recv.at[1],
        device_id=sibling,
        device_id_type=MESH,
    )
    back.start()

    @pl.loop(BATCHES // 2 + 1, last)
    def _(k):
        take_back(k)

    back.wait()
    save_wall = pltpu.make_async_copy(wall, wgrad, save_sem)
    save_act.wait()
    save_wall.start()
    wait_rows(returned, batch, recv2.at[last])
    picks, rows = picks_of(last), returned[span(last * batch, batch), :]
    saves = []
    for b in range(rows_own // tall):
        at = pl.ds(b * tall, tall)
        hid[at, :] = (acc[at, :] + hits(picks, rows, b)).astype(BF16)
        saves.append(pltpu.make_async_copy(hid.at[at], grad.at[at], load_sem.at[b]))
        saves[-1].start()
    wait_rows(returned, batch - slots, send2.at[0])

    @pl.loop(1, BATCHES)
    def _(k):
        wait_rows(returned, batch, send2.at[k])

    for save in saves:
        save.wait()
    save_wall.wait()


def deliver_kernel(act_in, grad_in, wgrad_in, act_out, grad_out, wgrad_out, act, grad, load_sem, save_sem):
    loads, saves = [], []
    for n, (src, via, dst) in enumerate(((act_in, act, act_out), (grad_in, grad, grad_out))):
        rows = src.shape[0] // PARTS
        for p in range(PARTS):
            at = pl.ds(p * rows, rows)
            loads.append(pltpu.make_async_copy(src.at[at], via.at[at], load_sem.at[n, p]))
            saves.append(pltpu.make_async_copy(via.at[at], dst.at[at], save_sem.at[n, p]))
    for load in loads:
        load.start()
    wgrad_out[...] = wgrad_in[...].astype(F32)
    for load, save in zip(loads, saves):
        load.wait()
        save.start()
    for save in saves:
        save.wait()


def per_device(features, weight, cotangent, tile_vals, tile_rows, tile_cols, send_rows, counts):
    rows_own, width = features.shape
    count = tile_vals.shape[0]
    slots = send_rows.shape[2]
    row_blocks = rows_own // EDGE
    remote_rows = DEVICES * slots
    cols_all = row_blocks + remote_rows // EDGE
    batch = 2 * SQUARE * slots

    any_ = pl.BlockSpec(memory_space=pl.ANY)
    vmem = pl.BlockSpec(memory_space=pltpu.VMEM)
    chips = DEVICES // 2
    edge_r = width * width // 2 // chips // EDGE
    dma = pltpu.SemaphoreType.DMA
    rows16 = pltpu.VMEM((rows_own, width), BF16)
    far16 = pltpu.VMEM((remote_rows, width), BF16)
    activated, grad, weight_grad = pl.pallas_call(
        network_kernel,
        out_shape=(
            jax.ShapeDtypeStruct((rows_own, width), BF16),
            jax.ShapeDtypeStruct((rows_own, width), BF16),
            jax.ShapeDtypeStruct((width, width), BF16),
        ),
        in_specs=[vmem] * 4 + [any_] * 4,
        out_specs=(any_,) * 3,
        scratch_shapes=[
            pltpu.VMEM((24, EDGE), jnp.int32),
            pltpu.SMEM((24, EDGE), jnp.int32),
            rows16,
            pltpu.VMEM((count + 1, EDGE, EDGE), BF16),
            pltpu.VMEM((count + 1, EDGE, EDGE), BF16),
            pltpu.VMEM((count + 1, EDGE, EDGE), BF16),
            pltpu.VMEM((width, width), BF16),
            rows16,
            pltpu.VMEM((DEVICES, EDGE), jnp.int32),
            pltpu.VMEM((SQUARES, SQUARE * slots), jnp.int32),
            far16,
            far16,
            pltpu.VMEM((rows_own, width), F32),
            rows16,
            rows16,
            rows16,
            far16,
            pltpu.VMEM((width, width), F32),
            pltpu.VMEM((width // 2, width), BF16),
            pltpu.VMEM((width // 2, width), F32),
            pltpu.VMEM((chips, edge_r, EDGE), BF16),
            pltpu.VMEM((edge_r, EDGE), BF16),
            pltpu.VMEM((width, width), BF16),
            dma((4,)),
            dma,
            dma((BATCHES,)),
            dma((BATCHES,)),
            dma((BATCHES,)),
            dma((BATCHES,)),
            dma((2,)),
            dma((2,)),
            dma,
            dma,
            dma,
            dma,
        ],
        compiler_params=pltpu.CompilerParams(
            collective_id=0, has_side_effects=True, vmem_limit_bytes=VMEM_LIMIT
        ),
        name="network",
    )(send_rows[0].T, counts, tile_rows.reshape(1, count), tile_cols.reshape(1, count), features, tile_vals, weight, cotangent)
    return pl.pallas_call(
        deliver_kernel,
        out_shape=(
            jax.ShapeDtypeStruct((rows_own, width), BF16),
            jax.ShapeDtypeStruct((rows_own, width), BF16),
            jax.ShapeDtypeStruct((width, width), F32),
        ),
        in_specs=[any_, any_, vmem],
        out_specs=(any_, any_, vmem),
        scratch_shapes=[rows16, rows16, dma((2, PARTS)), dma((2, PARTS))],
        compiler_params=pltpu.CompilerParams(vmem_limit_bytes=VMEM_LIMIT),
        name="deliver",
    )(activated, grad, weight_grad)


def solution(mesh):
    rows = P(("group", "local"), None)
    tiles = P(("group", "local"), None, None)
    flat = P(("group", "local"))
    return jax.shard_map(
        per_device,
        mesh=mesh,
        in_specs=(rows, P(), rows, tiles, flat, flat, tiles, rows),
        out_specs=(rows, rows, P()),
        check_vma=False,
    )
```

time: 157 us -> 140 us (0.89)
  Pallas kernels: 145 us -> 137 us
  local copies, waits for them, and re-layouts: 7.57 us -> 0 us
  other arithmetic: 2.23 us -> 0 us
    pallas_call x1, Pallas kernels: 145 us -> 131 us  [per_device(): pl.pallas_call(network_kernel, out_shape=(jax.ShapeDtypeStruct((rows_own,...]
    unnamed x8 -> x0, local copies, waits for them, and re-layouts: 7.57 us -> none
    pallas_call x0 -> x1, Pallas kernels: none -> 5.59 us  [per_device(): pl.pallas_call(deliver_kernel, out_shape=(jax.ShapeDtypeStruct((rows_own,...]
where the time goes in v3:
time: 140 us; the launch traced here: 138 us
  Pallas kernels  137 us (98%)
    pallas_call x1, Pallas kernels, per_device(): pl.pallas_call(network_kernel, out_shape=(jax.ShapeDtypeStruct((rows_own,...  131 us
    pallas_call x1, Pallas kernels, per_device(): pl.pallas_call(deliver_kernel, out_shape=(jax.ShapeDtypeStruct((rows_own,...  5.59 us

profile of v3, /device:TPU:39, one launch (start us, length us, event | category | flops | bytes accessed | tf_op | source)
XLA Modules:
  0.0 137.7 jit_solution(1012707990900055786)
XLA Ops:
  0.6 131.4 %network.1 = (bf16[2048,512]{1,0:T(8,128)(2,1)}, bf16[2048,512]{1,0:T(8,128)(2,1)}, bf16[512,512]{1,0:T(8,128)(2,1)}) custom-call(s32[32,128]{1,0:T(8,128)} %bitcast.5, s32[1,128]{1,0:T(1,128)} %live.1, s32[1,256]{1,0:T(1,128)} %bitcast.6, s32[1,256]{1,0:T(1,128)} %bitcast.7, bf16[2048,512]{1,0:T(8,128)(2,1)} %feat_in.1, bf16[256,128,128]{2,1,0:T(8,128)(2,1)} %vals.1, ...), custom_call_target="tpu_custom_call" | custom-call | tf_op jit(solution)/shard_map/network/pallas_call | solution.py:451
  132.0 5.6 %deliver.1 = (bf16[2048,512]{1,0:T(8,128)(2,1)}, bf16[2048,512]{1,0:T(8,128)(2,1)}, f32[512,512]{1,0:T(8,128)}) custom-call(bf16[2048,512]{1,0:T(8,128)(2,1)} %get-tuple-element.6.act_in, bf16[2048,512]{1,0:T(8,128)(2,1)} %get-tuple-element.7.grad_in, bf16[512,512]{1,0:T(8,128)(2,1)} %get-tuple-element.8.wgrad_in), custom_call_target="tpu_custom_call" | custom-call | tf_op jit(solution)/shard_map/deliver/pallas_call | solution.py:502

commit v4 on v3

--- a/solution.py
+++ b/solution.py
@@ -318,7 +318,7 @@
         give(k)
         send_batch(k, returned, send2, recv2)
 
-    @pl.loop(2, BATCHES // 2)
+    @pl.loop(2, BATCHES)
     def _(k):
         give_batch(k)
 
@@ -343,9 +343,6 @@
             device_id_type=MESH,
         ).start()
 
-    @pl.loop(BATCHES // 2, BATCHES)
-    def _(k):
-        give_batch(k)
 
     tall = 1024
 
@@ -371,7 +368,7 @@
     wait_rows(returned, batch - slots, recv2.at[0])
     add_batch(0)
 
-    @pl.loop(1, BATCHES // 2 + 1)
+    @pl.loop(1, last - 1)
     def _(k):
         take_back(k)
 
@@ -387,7 +384,7 @@
     )
     back.start()
 
-    @pl.loop(BATCHES // 2 + 1, last)
+    @pl.loop(last - 1, last)
     def _(k):
         take_back(k)
 
@@ -414,7 +411,7 @@
     save_wall.wait()
 
 
-def deliver_kernel(act_in, grad_in, wgrad_in, act_out, grad_out, wgrad_out, act, grad, load_sem, save_sem):
+def deliver_kernel(act_in, grad_in, wgrad_in, act_out, grad_out, wgrad_out, act, grad, small, wide, load_sem, save_sem):
     loads, saves = [], []
     for n, (src, via, dst) in enumerate(((act_in, act, act_out), (grad_in, grad, grad_out))):
         rows = src.shape[0] // PARTS
@@ -422,14 +419,20 @@
             at = pl.ds(p * rows, rows)
             loads.append(pltpu.make_async_copy(src.at[at], via.at[at], load_sem.at[n, p]))
             saves.append(pltpu.make_async_copy(via.at[at], dst.at[at], save_sem.at[n, p]))
+    load_small = pltpu.make_async_copy(wgrad_in, small, load_sem.at[2, 0])
+    save_wide = pltpu.make_async_copy(wide, wgrad_out, save_sem.at[2, 0])
+    load_small.start()
     for load in loads:
         load.start()
-    wgrad_out[...] = wgrad_in[...].astype(F32)
+    load_small.wait()
+    wide[...] = small[...].astype(F32)
+    save_wide.start()
     for load, save in zip(loads, saves):
         load.wait()
         save.start()
     for save in saves:
         save.wait()
+    save_wide.wait()
 
 
 def per_device(features, weight, cotangent, tile_vals, tile_rows, tile_cols, send_rows, counts):
@@ -506,9 +509,16 @@
             jax.ShapeDtypeStruct((rows_own, width), BF16),
             jax.ShapeDtypeStruct((width, width), F32),
         ),
-        in_specs=[any_, any_, vmem],
-        out_specs=(any_, any_, vmem),
-        scratch_shapes=[rows16, rows16, dma((2, PARTS)), dma((2, PARTS))],
+        in_specs=[any_] * 3,
+        out_specs=(any_,) * 3,
+        scratch_shapes=[
+            rows16,
+            rows16,
+            pltpu.VMEM((width, width), BF16),
+            pltpu.VMEM((width, width), F32),
+            dma((3, PARTS)),
+            dma((3, PARTS)),
+        ],
         compiler_params=pltpu.CompilerParams(vmem_limit_bytes=VMEM_LIMIT),
         name="deliver",
     )(activated, grad, weight_grad)

time: 140 us -> 137 us (0.979); the launches traced: 138 us -> 137 us
    pallas_call x1, Pallas kernels: 5.59 us -> 4.05 us  [per_device(): pl.pallas_call(deliver_kernel, out_shape=(jax.ShapeDtypeStruct((rows_own,...]
where the time goes in v4:
time: 137 us
  Pallas kernels  136 us (99%)
    pallas_call x1, Pallas kernels, per_device(): pl.pallas_call(network_kernel, out_shape=(jax.ShapeDtypeStruct((rows_own,...  132 us
    pallas_call x1, Pallas kernels, per_device(): pl.pallas_call(deliver_kernel, out_shape=(jax.ShapeDtypeStruct((rows_own,...  4.05 us

profile of v4, /device:TPU:39, one launch (start us, length us, event | category | flops | bytes accessed | tf_op | source)
XLA Modules:
  0.0 136.9 jit_solution(3572875748074196305)
XLA Ops:
  0.6 132.1 %network.1 = (bf16[2048,512]{1,0:T(8,128)(2,1)}, bf16[2048,512]{1,0:T(8,128)(2,1)}, bf16[512,512]{1,0:T(8,128)(2,1)}) custom-call(s32[32,128]{1,0:T(8,128)} %bitcast.5, s32[1,128]{1,0:T(1,128)} %live.1, s32[1,256]{1,0:T(1,128)} %bitcast.6, s32[1,256]{1,0:T(1,128)} %bitcast.7, bf16[2048,512]{1,0:T(8,128)(2,1)} %feat_in.1, bf16[256,128,128]{2,1,0:T(8,128)(2,1)} %vals.1, ...), custom_call_target="tpu_custom_call" | custom-call | tf_op jit(solution)/shard_map/network/pallas_call | solution.py:454
  132.7 4.0 %deliver.1 = (bf16[2048,512]{1,0:T(8,128)(2,1)}, bf16[2048,512]{1,0:T(8,128)(2,1)}, f32[512,512]{1,0:T(8,128)}) custom-call(bf16[2048,512]{1,0:T(8,128)(2,1)} %get-tuple-element.6.act_in, bf16[2048,512]{1,0:T(8,128)(2,1)} %get-tuple-element.7.grad_in, bf16[512,512]{1,0:T(8,128)(2,1)} %get-tuple-element.8.wgrad_in), custom_call_target="tpu_custom_call" | custom-call | tf_op jit(solution)/shard_map/deliver/pallas_call | solution.py:505

commit v5 on v4

--- a/solution.py
+++ b/solution.py
@@ -297,9 +297,20 @@
     def mate(q):
         return device(div(q, SIDE), rem(q, SIDE) * 2 + core)
 
-    @pl.loop(1, chips)
-    def _(k):
-        q = rem(chip + k, chips)
+    def to_mates(put):
+        def squares(k, skip):
+            for dy in (2, 3, 0, 1):
+                for a in (0, 1):
+                    if not (skip and (a, dy) == (0, 0)):
+                        put(square_of(k, a, 1) * SIDE + rem(y + dy, SIDE))
+
+        squares(0, True)
+
+        @pl.loop(1, BATCHES)
+        def _(k):
+            squares(k, False)
+
+    def scatter_part(q):
         r0, c0 = spot(q)
         pltpu.make_async_remote_copy(
             src_ref=wsum.at[span(r0, edge_r), span(c0, edge_c)],
@@ -310,6 +321,7 @@
             device_id_type=MESH,
         ).start()
 
+    to_mates(scatter_part)
     r0, c0 = spot(chip)
     chunks[chip] = wsum[span(r0, edge_r), span(c0, edge_c)]
 
@@ -318,7 +330,7 @@
         give(k)
         send_batch(k, returned, send2, recv2)
 
-    @pl.loop(2, BATCHES)
+    @pl.loop(2, BATCHES - 2)
     def _(k):
         give_batch(k)
 
@@ -332,17 +344,21 @@
     there = (span(mine + r0, edge_r), span(c0, edge_c))
     wall[there[0], there[1]] = gathered[...]
 
-    @pl.loop(1, chips)
-    def _(k):
+    def share_sum(q):
         pltpu.make_async_remote_copy(
             src_ref=gathered,
             dst_ref=wall.at[there[0], there[1]],
             send_sem=ag_send,
             recv_sem=ag_recv,
-            device_id=mate(rem(chip + k, chips)),
+            device_id=mate(q),
             device_id_type=MESH,
         ).start()
 
+    to_mates(share_sum)
+
+    @pl.loop(BATCHES - 2, BATCHES)
+    def _(k):
+        give_batch(k)
 
     tall = 1024
 

time: 137 us -> 138 us (level)
  no operation moved by 1% of the time
where the time goes in v5:
time: 138 us
  Pallas kernels  137 us (99%)
    pallas_call x1, Pallas kernels, per_device(): pl.pallas_call(network_kernel, out_shape=(jax.ShapeDtypeStruct((rows_own,...  133 us
    pallas_call x1, Pallas kernels, per_device(): pl.pallas_call(deliver_kernel, out_shape=(jax.ShapeDtypeStruct((rows_own,...  4.05 us

profile of v5, /device:TPU:39, one launch (start us, length us, event | category | flops | bytes accessed | tf_op | source)
XLA Modules:
  0.0 138.0 jit_solution(405199783409465044)
XLA Ops:
  0.6 133.1 %network.1 = (bf16[2048,512]{1,0:T(8,128)(2,1)}, bf16[2048,512]{1,0:T(8,128)(2,1)}, bf16[512,512]{1,0:T(8,128)(2,1)}) custom-call(s32[32,128]{1,0:T(8,128)} %bitcast.5, s32[1,128]{1,0:T(1,128)} %live.1, s32[1,256]{1,0:T(1,128)} %bitcast.6, s32[1,256]{1,0:T(1,128)} %bitcast.7, bf16[2048,512]{1,0:T(8,128)(2,1)} %feat_in.1, bf16[256,128,128]{2,1,0:T(8,128)(2,1)} %vals.1, ...), custom_call_target="tpu_custom_call" | custom-call | tf_op jit(solution)/shard_map/network/pallas_call | solution.py:470
  133.8 4.0 %deliver.1 = (bf16[2048,512]{1,0:T(8,128)(2,1)}, bf16[2048,512]{1,0:T(8,128)(2,1)}, f32[512,512]{1,0:T(8,128)}) custom-call(bf16[2048,512]{1,0:T(8,128)(2,1)} %get-tuple-element.6.act_in, bf16[2048,512]{1,0:T(8,128)(2,1)} %get-tuple-element.7.grad_in, bf16[512,512]{1,0:T(8,128)(2,1)} %get-tuple-element.8.wgrad_in), custom_call_target="tpu_custom_call" | custom-call | tf_op jit(solution)/shard_map/deliver/pallas_call | solution.py:521
